TPU v7x, 32 devices: a whole 2x2x4 slice. The times are simulated.
32 devices in a mesh: row: 8 (over z, core), col: 4 (over y, x).
Axes of the slice: x: 2, y: 2, z: 4, core: 2. Of those that a mesh axis runs over, the one named last changes fastest.
Arguments:
- demo: bfloat16 [8192, 256], P(('row', 'col'))
- rollout: bfloat16 [8192, 256], P(('row', 'col'))
Outputs:
- demo_potential: float32 [8192], P(('row', 'col'))
- rollout_potential: float32 [8192], P(('row', 'col'))
- rollout_reward: float32 [8192], P(('row', 'col'))
All inputs are finite; a program needn't handle non-finite values.
Results may differ from a plain program's by a relative error of at most 0.0065.
The roundings to bfloat16 on the way count: a program that leaves them out, or rounds other values in their place, can miss the bound.
Values may be sent and summed in bfloat16 or wider, within the bound.
A program may use at most 64 MiB of HBM per device.

v0:
```python
import math

import jax
import jax.numpy as jnp
from jax import lax
from jax.sharding import PartitionSpec as P

ITERS = 2


EPS = 0.005


def normalize(embed):
    values = embed.astype(jnp.float32)
    inverse = lax.rsqrt(jnp.sum(values * values, axis=-1, keepdims=True) + 1e-06)
    return (values * inverse).astype(jnp.bfloat16)


def cost_of(left, right):
    inner = lax.dot_general(
        left, right, (((1,), (1,)), ((), ())), preferred_element_type=jnp.float32
    )
    return 1.0 - inner


def over_columns(expo):
    top = jnp.max(expo, axis=1)
    top = lax.pmax(top, "col")
    total = lax.psum(jnp.sum(jnp.exp(expo - top[:, None]), axis=1), "col")
    return top + jnp.log(total)


def over_rows(expo):
    top = jnp.max(expo, axis=0)
    top = lax.pmax(top, "row")
    total = lax.psum(jnp.sum(jnp.exp(expo - top[None, :]), axis=0), "row")
    return top + jnp.log(total)


def body(demo, rollout):
    demo_unit = lax.all_gather(normalize(demo), "col", axis=0, tiled=True)
    rollout_unit = lax.all_gather(normalize(rollout), "row", axis=0, tiled=True)
    rows_here = demo_unit.shape[0]
    cols_here = rollout_unit.shape[0]
    total_rows = rows_here * lax.axis_size("row")
    total_cols = cols_here * lax.axis_size("col")
    log_rows = -math.log(total_rows)
    log_cols = -math.log(total_cols)
    stored = cost_of(demo_unit, rollout_unit)

    def get_tile():
        return stored

    g_pot = jnp.zeros((cols_here,), jnp.float32)
    f_pot = jnp.zeros((rows_here,), jnp.float32)
    for step in range(ITERS):
        f_pot = EPS * log_rows - EPS * over_columns((g_pot[None, :] - get_tile()) / EPS)
        g_pot = EPS * log_cols - EPS * over_rows((f_pot[:, None] - get_tile()) / EPS)
    tile = get_tile()
    plan = jnp.exp((f_pot[:, None] + g_pot[None, :] - tile) / EPS)
    weighted = lax.psum(jnp.sum(plan * tile, axis=0), "row")
    reward = -float(total_cols) * weighted
    row_share = rows_here // lax.axis_size("col")
    col_share = cols_here // lax.axis_size("row")
    demo_out = lax.dynamic_slice_in_dim(f_pot / EPS, lax.axis_index("col") * row_share, row_share)
    rollout_out = lax.dynamic_slice_in_dim(
        g_pot / EPS, lax.axis_index("row") * col_share, col_share
    )
    reward_out = lax.dynamic_slice_in_dim(reward, lax.axis_index("row") * col_share, col_share)
    return (demo_out, rollout_out, reward_out)


def solution(mesh):
    return jax.shard_map(
        body,
        mesh=mesh,
        in_specs=(P(("row", "col"), None), P(("row", "col"), None)),
        out_specs=(P(("row", "col")), P(("row", "col")), P(("row", "col"))),
        check_vma=False,
    )
```

profile of v0, /device:TPU:0, one launch (start us, length us, event | category | flops | bytes accessed | tf_op | source)
XLA Modules:
  0.0 191.0 jit_solution(16344978116320516850)
XLA Ops:
  7.2 0.0 all-gather.2.cloned.1.call-start
  7.2 1.0 fusion.6
  8.2 1.6 fusion.7
  9.9 0.0 all-gather.2.cloned.1.call-update
  9.9 1.0 fusion.4
  11.0 1.0 fusion.5
  12.0 11.5 %all_gather.6 = bf16[1024,256]{1,0:T(8,128)(2,1)S(1)} all-gather(bf16[256,256]{1,0:T(8,128)(2,1)S(1)} %fusion.5), channel_id=1, replica_groups=mesh['row'=8,'col'=4] {'col'}, dimensions={0}, use_global_device_ids=true | all-gather | bytes 655360 | tf_op jit(solution)/shard_map/all_gather | solution.py:42
  23.5 11.4 %all-gather.2.cloned.1.call-done = bf16[2048,256]{1,0:T(8,128)(2,1)} async-done(((bf16[256,256]{1,0:T(8,128)(2,1)}), bf16[2048,256]{1,0:T(8,128)(2,1)}) %all-gather.2.cloned.1.call-update) | async-done | bytes 1048592 | tf_op jit(solution)/shard_map/all_gather | solution.py:43
  34.9 5.7 %fusion = (f32[1024]{0:T(1024)S(1)}, f32[1024,2048]{1,0:T(8,128)}) fusion(bf16[1024,256]{1,0:T(8,128)(2,1)S(1)} %all_gather.6, bf16[2048,256]{1,0:T(8,128)(2,1)} %all-gather.2.cloned.1.call-done), kind=kOutput, calls=%fused_computation.9 | convolution fusion | flops 1082129408 | bytes 9965568 | tf_op jit(solution)/shard_map/dot_general | solution.py:21
  40.6 9.8 %pmax.28 = f32[1024]{0:T(1024)S(1)} all-reduce(f32[1024]{0:T(1024)S(1)} %get-tuple-element.5), channel_id=1, replica_groups=mesh['row'=8,'col'=4] {'col'}, use_global_device_ids=true, to_apply=%region_3.0 | all-reduce | flops 1024 | bytes 8192 | tf_op jit(solution)/shard_map/pmax | solution.py:29
  50.4 4.6 %exponential_reduce_fusion.3 = f32[1024]{0:T(1024)S(1)} fusion(f32[1024,2048]{1,0:T(8,128)} %get-tuple-element.6, f32[1024]{0:T(1024)S(1)} %pmax.28), kind=kLoop, calls=%fused_computation.7 | loop fusion | flops 10484736 | bytes 8396800 | tf_op jit(solution)/shard_map/reduce_sum | solution.py:30
  55.0 8.0 %psum.35 = f32[1024]{0:T(1024)S(1)} all-reduce(f32[1024]{0:T(1024)S(1)} %exponential_reduce_fusion.3), channel_id=1, replica_groups=mesh['row'=8,'col'=4] {'col'}, use_global_device_ids=true, to_apply=%region_5.0 | all-reduce | flops 1024 | bytes 8192 | tf_op jit(solution)/shard_map/psum | solution.py:30
  63.0 4.5 %fusion.1 = f32[2048]{0:T(1024)S(1)} fusion(f32[1024,2048]{1,0:T(8,128)} %get-tuple-element.6, f32[1024]{0:T(1024)S(1)} %multiply_subtract_fusion.3), kind=kLoop, calls=%fused_computation.10 | loop fusion | flops 8386560 | bytes 8400896 | tf_op jit(solution)/shard_map/reduce_max | solution.py:35
  67.6 13.8 %pmax.29 = f32[2048]{0:T(1024)S(1)} all-reduce(f32[2048]{0:T(1024)S(1)} %fusion.1), channel_id=1, replica_groups=mesh['row'=8,'col'=4] {'row'}, use_global_device_ids=true, to_apply=%region_7.0 | all-reduce | flops 2048 | bytes 16384 | tf_op jit(solution)/shard_map/pmax | solution.py:36
  81.4 4.6 %exponential_reduce_fusion.2 = f32[2048]{0:T(1024)S(1)} fusion(f32[1024,2048]{1,0:T(8,128)} %get-tuple-element.6, f32[2048]{0:T(1024)S(1)} %pmax.29, f32[1024]{0:T(1024)S(1)} %multiply_subtract_fusion.3), kind=kLoop, calls=%fused_computation.5 | loop fusion | flops 10483712 | bytes 8409088 | tf_op jit(solution)/shard_map/reduce_sum | solution.py:37
  86.1 13.9 %psum.36 = f32[2048]{0:T(1024)S(1)} all-reduce(f32[2048]{0:T(1024)S(1)} %exponential_reduce_fusion.2), channel_id=1, replica_groups=mesh['row'=8,'col'=4] {'row'}, use_global_device_ids=true, to_apply=%region_9.0 | all-reduce | flops 2048 | bytes 16384 | tf_op jit(solution)/shard_map/psum | solution.py:37
  100.0 4.5 %fusion.2 = f32[1024]{0:T(1024)S(1)} fusion(f32[1024,2048]{1,0:T(8,128)} %get-tuple-element.6, f32[2048]{0:T(1024)S(1)} %multiply_subtract_fusion.1), kind=kLoop, calls=%fused_computation.11 | loop fusion | flops 8387584 | bytes 8400896 | tf_op jit(solution)/shard_map/reduce_max | solution.py:28
  104.6 9.0 %pmax.30 = f32[1024]{0:T(1024)S(1)} all-reduce(f32[1024]{0:T(1024)S(1)} %fusion.2), channel_id=1, replica_groups=mesh['row'=8,'col'=4] {'col'}, use_global_device_ids=true, to_apply=%region_11.0 | all-reduce | flops 1024 | bytes 8192 | tf_op jit(solution)/shard_map/pmax | solution.py:29
  113.5 4.6 %exponential_reduce_fusion.1 = f32[1024]{0:T(1024)S(1)} fusion(f32[1024,2048]{1,0:T(8,128)} %get-tuple-element.6, f32[1024]{0:T(1024)S(1)} %pmax.30, f32[2048]{0:T(1024)S(1)} %multiply_subtract_fusion.1), kind=kLoop, calls=%fused_computation.3 | loop fusion | flops 10484736 | bytes 8404992 | tf_op jit(solution)/shard_map/reduce_sum | solution.py:30
  118.2 8.0 %psum.37 = f32[1024]{0:T(1024)S(1)} all-reduce(f32[1024]{0:T(1024)S(1)} %exponential_reduce_fusion.1), channel_id=1, replica_groups=mesh['row'=8,'col'=4] {'col'}, use_global_device_ids=true, to_apply=%region_13.0 | all-reduce | flops 1024 | bytes 8192 | tf_op jit(solution)/shard_map/psum | solution.py:30
  126.2 4.5 %fusion.3 = f32[2048]{0:T(1024)S(1)} fusion(f32[1024,2048]{1,0:T(8,128)} %get-tuple-element.6, f32[1024]{0:T(1024)S(1)} %get-tuple-element.4), kind=kLoop, calls=%fused_computation.12 | loop fusion | flops 8386560 | bytes 8400896 | tf_op jit(solution)/shard_map/reduce_max | solution.py:35
  130.7 13.9 %pmax.31 = f32[2048]{0:T(1024)S(1)} all-reduce(f32[2048]{0:T(1024)S(1)} %fusion.3), channel_id=1, replica_groups=mesh['row'=8,'col'=4] {'row'}, use_global_device_ids=true, to_apply=%region_15.0 | all-reduce | flops 2048 | bytes 16384 | tf_op jit(solution)/shard_map/pmax | solution.py:36
  144.7 4.6 %exponential_reduce_fusion = f32[2048]{0:T(1024)S(1)} fusion(f32[1024,2048]{1,0:T(8,128)} %get-tuple-element.6, f32[2048]{0:T(1024)S(1)} %pmax.31, f32[1024]{0:T(1024)S(1)} %get-tuple-element.4), kind=kLoop, calls=%fused_computation.1 | loop fusion | flops 10483712 | bytes 8409088 | tf_op jit(solution)/shard_map/reduce_sum | solution.py:37
  149.3 13.9 %psum.38 = f32[2048]{0:T(1024)S(1)} all-reduce(f32[2048]{0:T(1024)S(1)} %exponential_reduce_fusion), channel_id=1, replica_groups=mesh['row'=8,'col'=4] {'row'}, use_global_device_ids=true, to_apply=%region_17.0 | all-reduce | flops 2048 | bytes 16384 | tf_op jit(solution)/shard_map/psum | solution.py:37
  163.2 5.1 %multiply_reduce_fusion = f32[2048]{0:T(1024)S(1)} fusion(f32[1024,2048]{1,0:T(8,128)} %get-tuple-element.6, f32[2048]{0:T(1024)S(1)} %multiply_subtract_fusion, f32[1024]{0:T(1024)S(1)} %get-tuple-element.4), kind=kLoop, calls=%fused_computation | loop fusion | flops 12580864 | bytes 8409088 | tf_op jit(solution)/shard_map/reduce_sum | solution.py:62
  168.4 13.9 %psum.39 = f32[2048]{0:T(1024)S(1)} all-reduce(f32[2048]{0:T(1024)S(1)} %multiply_reduce_fusion), channel_id=1, replica_groups=mesh['row'=8,'col'=4] {'row'}, use_global_device_ids=true, to_apply=%region_19.0 | all-reduce | flops 2048 | bytes 16384 | tf_op jit(solution)/shard_map/psum | solution.py:62
  182.3 0.6 dynamic-slice_multiply_fusion.1
  182.9 0.6 dynamic-slice_multiply_fusion
  183.6 0.6 dynamic_slice.9
  (6 shorter events, 0.1 us)
Async XLA Ops:
  7.2 27.7 %all-gather.2.cloned.1.call-start = ((), (), s32[]{:S(2)}) async-start(), calls=%async_computation | async-start | bytes 1179648 | tf_op jit(solution)/shard_map/all_gather | solution.py:43
Sparse Core Ops, SparseCore 0:
  10.0 24.7 all-gather.1
where the time goes:
time: 192 us; the launch traced here: 191 us
  blocking collectives  116 us (60%)
  other arithmetic  43.2 us (22%)
  between operations  14.2 us (7%)
  waiting for transfers between devices  11.4 us (6%)
  matrix products  5.75 us (3%)
    psum x2, blocking collectives, over_rows(): total = lax.psum(jnp.sum(jnp.exp(expo - top[None, :]), axis=0), 'row')  27.8 us
    pmax x2, blocking collectives, over_rows(): top = lax.pmax(top, 'row')  27.8 us
    pmax x2, blocking collectives, over_columns(): top = lax.pmax(top, 'col')  18.8 us
    psum x2, blocking collectives, over_columns(): total = lax.psum(jnp.sum(jnp.exp(expo - top[:, None]), axis=1), 'col')  16 us
    psum x1, blocking collectives, body(): weighted = lax.psum(jnp.sum(plan * tile, axis=0), 'row')  13.9 us
    all_gather x1, blocking collectives, body(): demo_unit = lax.all_gather(normalize(demo), 'col', axis=0, tiled=True)  11.5 us
    all_gather x1, waiting for transfers between devices, body(): rollout_unit = lax.all_gather(normalize(rollout), 'row', axis=0, tiled=True)  11.4 us
    reduce_sum x2, other arithmetic, over_rows(): total = lax.psum(jnp.sum(jnp.exp(expo - top[None, :]), axis=0), 'row')  9.26 us
  transfers between devices with their start and end apart: 1, of which 1 were waited for; matrix products, arithmetic and copies ran while one was open for 1% of the time, Pallas kernels for 0%

commit v1 on v0

v1 whole, which is shorter than its diff:
```python
import functools
import math

import jax
import jax.numpy as jnp
from jax import lax
from jax.experimental import pallas as pl
from jax.experimental.pallas import tpu as pltpu
from jax.sharding import PartitionSpec as P

EPS = 0.005
MESH = pl.DeviceIdType.MESH
LANES = 128
SUB = 8


class Plan:
    def __init__(self, rows_axis, cols_axis, blk, width):
        self.core = 2
        depth = rows_axis // 2
        self.x = 1 << ((cols_axis.bit_length() - 1) // 2)
        self.y = cols_axis // self.x
        self.zl = min(depth, max(1, cols_axis // self.x))
        self.zh = depth // self.zl
        self.blk = blk
        self.width = width
        self.gr = self.zl * self.x
        self.gc = self.zh * self.y * self.core
        self.rows = self.gr * blk
        self.cols = self.gc * blk
        self.total = rows_axis * cols_axis * blk
        self.pieces = max(1, min(4, blk // 16))
        self.piece = blk // self.pieces


def normalize(embed):
    values = embed.astype(jnp.float32)
    inverse = lax.rsqrt(jnp.sum(values * values, axis=-1, keepdims=True) + 1e-06)
    return (values * inverse).astype(jnp.bfloat16)


def tree(op, items):
    items = list(items)
    while len(items) > 1:
        items = [
            op(items[i], items[i + 1]) if i + 1 < len(items) else items[i]
            for i in range(0, len(items), 2)
        ]
    return items[0]


def kernel(
    plan,
    demo_ref,
    roll_ref,
    fo_ref,
    go_ref,
    ro_ref,
    dem,
    rol,
    dist,
    kern,
    best,
    part,
    wide,
    scale,
    lf1,
    lf2,
    lg,
    f_own,
    g_own,
    cw_out,
    cw_in,
    s_dem,
    r_dem,
    s_rol,
    r_rol,
    s_f1,
    r_f1,
    s_f2,
    r_f2,
    s_g,
    r_g,
    s_c,
    r_c,
):
    blk, rows, cols = plan.blk, plan.rows, plan.cols
    n_parts = cols // LANES
    n_groups = rows // SUB
    row = lax.axis_index("row")
    col = lax.axis_index("col")
    core, z = lax.rem(row, 2), row // 2
    zlo, zhi = lax.rem(z, plan.zl), z // plan.zl
    x, y = lax.rem(col, plan.x), col // plan.x

    def row_peer(dz, dx):
        zz, xx = lax.rem(zlo + dz, plan.zl), lax.rem(x + dx, plan.x)
        device = ((zhi * plan.zl + zz) * 2 + core, y * plan.x + xx)
        return device, zz * plan.x + xx

    def col_peer(dz, dy, dc):
        zz, yy, cc = lax.rem(zhi + dz, plan.zh), lax.rem(y + dy, plan.y), lax.rem(core + dc, 2)
        device = ((zz * plan.zl + zlo) * 2 + cc, yy * plan.x + x)
        return device, (zz * plan.y + yy) * 2 + cc

    row_offsets = [(a, b) for a in range(plan.zl) for b in range(plan.x)]
    col_offsets = [(a, b, c) for a in range(plan.zh) for b in range(plan.y) for c in range(2)]
    row_peers = {o: row_peer(*o) for o in row_offsets}
    col_peers = {o: col_peer(*o) for o in col_offsets}
    p_me = row_peers[(0, 0)][1]
    q_me = col_peers[(0, 0, 0)][1]
    row_others = [row_peers[o] for o in row_offsets[1:]]
    col_others = [col_peers[o] for o in col_offsets[1:]]

    barrier = pltpu.get_barrier_semaphore()
    for device, _ in row_others + col_others:
        pl.semaphore_signal(barrier, inc=1, device_id=device, device_id_type=MESH)

    def slot(buf, index, piece):
        start = pl.multiple_of(index * blk + piece * plan.piece, 16)
        return buf.at[pl.ds(start, plan.piece), :]

    dem[pl.ds(pl.multiple_of(p_me * blk, 16), blk), :] = normalize(demo_ref[...])
    rol[pl.ds(pl.multiple_of(q_me * blk, 16), blk), :] = normalize(roll_ref[...])
    pl.semaphore_wait(barrier, len(row_others) + len(col_others))

    partner = col_peers[(0, 0, 1)][0]
    started = []

    def send(buf, index, piece, device, ssem, rsem, count):
        ref = slot(buf, index, piece)
        copy = pltpu.make_async_remote_copy(
            src_ref=ref,
            dst_ref=ref,
            send_sem=ssem.at[count[0]],
            recv_sem=rsem.at[index, piece],
            device_id=device,
            device_id_type=MESH,
        )
        copy.start()
        count[0] += 1
        started.append(copy)

    def arrived(buf, index, piece, ssem, rsem):
        ref = slot(buf, index, piece)
        pltpu.make_async_remote_copy(
            src_ref=ref,
            dst_ref=ref,
            send_sem=ssem.at[0],
            recv_sem=rsem.at[index, piece],
            device_id=partner,
            device_id_type=MESH,
        ).wait_recv()

    n_dem, n_rol = [0], [0]
    send_dem = lambda i, k, d: send(dem, i, k, d, s_dem, r_dem, n_dem)
    send_rol = lambda i, k, d: send(rol, i, k, d, s_rol, r_rol, n_rol)
    for k in range(plan.pieces):
        for dz in range(1, plan.zl):
            send_dem(p_me, k, row_peers[(dz, 0)][0])
        for dz in range(1, plan.zh):
            send_rol(q_me, k, col_peers[(dz, 0, 0)][0])
        for dx in range(1, plan.x):
            send_dem(p_me, k, row_peers[(0, dx)][0])
        for dy in range(1, plan.y):
            send_rol(q_me, k, col_peers[(0, dy, 0)][0])
        send_rol(q_me, k, col_peers[(0, 0, 1)][0])
    for k in range(plan.pieces):
        for dz in range(1, plan.zl):
            index = row_peers[(dz, 0)][1]
            arrived(dem, index, k, s_dem, r_dem)
            for dx in range(1, plan.x):
                send_dem(index, k, row_peers[(0, dx)][0])
        for dz in range(1, plan.zh):
            index = col_peers[(dz, 0, 0)][1]
            arrived(rol, index, k, s_rol, r_rol)
            for dy in range(1, plan.y):
                send_rol(index, k, col_peers[(0, dy, 0)][0])
            send_rol(index, k, partner)
        for dy in range(1, plan.y):
            index = col_peers[(0, dy, 0)][1]
            arrived(rol, index, k, s_rol, r_rol)
            send_rol(index, k, partner)
    for k in range(plan.pieces):
        for dz in range(1, plan.zh):
            for dy in range(1, plan.y):
                index = col_peers[(dz, dy, 0)][1]
                arrived(rol, index, k, s_rol, r_rol)
                send_rol(index, k, partner)
    for k in range(plan.pieces):
        for dz in range(plan.zl):
            for dx in range(1, plan.x):
                arrived(dem, row_peers[(dz, dx)][1], k, s_dem, r_dem)
        for dz in range(plan.zh):
            for dy in range(plan.y):
                arrived(rol, col_peers[(dz, dy, 1)][1], k, s_rol, r_rol)

    step = 2 * LANES
    for c in range(cols // step):
        inner = lax.dot_general(
            dem[...],
            rol[c * step : (c + 1) * step, :],
            (((1,), (1,)), ((), ())),
            preferred_element_type=jnp.float32,
        )
        dist[:, c * step : (c + 1) * step] = (1.0 - inner) * (1.0 / EPS)

    def lanes(c):
        return slice(c * LANES, (c + 1) * LANES)

    def group(r):
        return pl.ds(pl.multiple_of(r * SUB, SUB), SUB)

    eye = lax.broadcasted_iota(jnp.int32, (LANES, LANES), 0) == lax.broadcasted_iota(
        jnp.int32, (LANES, LANES), 1
    )

    def to_lanes(column):
        return jnp.sum(jnp.where(eye, column, 0.0), axis=0, keepdims=True)

    def spread(line):
        for k in range(rows // LANES):
            column = jnp.sum(jnp.where(eye, line[:, lanes(k)], 0.0), axis=1, keepdims=True)
            wide[lanes(k), :] = jnp.broadcast_to(column, (LANES, LANES))

    def exchange(buf, index, others, ssem, rsem):
        copies = [
            pltpu.make_async_remote_copy(
                src_ref=buf.at[index],
                dst_ref=buf.at[index],
                send_sem=ssem.at[i],
                recv_sem=rsem.at[index],
                device_id=device,
                device_id_type=MESH,
            )
            for i, (device, _) in enumerate(others)
        ]
        for copy in copies:
            copy.start()
        started.extend(copies)
        for i, (device, other) in enumerate(others):
            pltpu.make_async_remote_copy(
                src_ref=buf.at[other],
                dst_ref=buf.at[other],
                send_sem=ssem.at[i],
                recv_sem=rsem.at[other],
                device_id=device,
                device_id_type=MESH,
            ).wait_recv()

    def log_total(buf, count):
        values = [buf[i] for i in range(count)]
        top = tree(jnp.maximum, values)
        return top + jnp.log(tree(jnp.add, [jnp.exp(v - top) for v in values]))

    log_n = math.log(plan.total)

    def first_rows(r, carry):
        here = group(r)
        values = [dist[here, lanes(c)] for c in range(n_parts)]
        low = tree(jnp.minimum, values)
        best[here, :] = low
        part[here, :] = tree(jnp.add, [jnp.exp(low - v) for v in values])
        return carry

    lax.fori_loop(0, n_groups, first_rows, 0, unroll=4)
    for k in range(rows // LANES):
        low = best[lanes(k), :]
        least = jnp.min(low, axis=1, keepdims=True)
        total = jnp.sum(part[lanes(k), :] * jnp.exp(least - low), axis=1, keepdims=True)
        lf1[p_me, :, lanes(k)] = jnp.log(to_lanes(total)) - to_lanes(least)
    exchange(lf1, p_me, row_others, s_f1, r_f1)
    f_line = -log_n - log_total(lf1, plan.gr)
    spread(f_line)

    def col_max(r, carry):
        here = group(r)
        f_here = wide[here, :]
        return tuple(
            jnp.maximum(carry[c], f_here - dist[here, lanes(c)]) for c in range(n_parts)
        )

    tops = lax.fori_loop(
        0,
        n_groups,
        col_max,
        tuple(jnp.full((SUB, LANES), -jnp.inf, jnp.float32) for _ in range(n_parts)),
        unroll=4,
    )

    def col_sum(r, carry):
        here = group(r)
        f_here = wide[here, :]
        out = []
        for c in range(n_parts):
            value = jnp.exp((f_here - dist[here, lanes(c)]) - tops[c])
            kern[here, lanes(c)] = value
            out.append(carry[c] + value)
        return tuple(out)

    zeros = tuple(jnp.zeros((SUB, LANES), jnp.float32) for _ in range(n_parts))
    sums = lax.fori_loop(0, n_groups, col_sum, zeros, unroll=4)
    for c in range(n_parts):
        top = jnp.max(tops[c], axis=0, keepdims=True)
        total = jnp.sum(sums[c] * jnp.exp(tops[c] - top), axis=0, keepdims=True)
        lg[q_me, :, lanes(c)] = top + jnp.log(total)
    exchange(lg, q_me, col_others, s_g, r_g)
    g_line = -log_n - log_total(lg, plan.gc)
    for c in range(n_parts):
        scale[:, lanes(c)] = jnp.exp(tops[c] + g_line[:, lanes(c)])

    def second_rows(r, carry):
        here = group(r)
        part[here, :] = tree(
            jnp.add, [kern[here, lanes(c)] * scale[:, lanes(c)] for c in range(n_parts)]
        )
        return carry

    lax.fori_loop(0, n_groups, second_rows, 0, unroll=4)
    for k in range(rows // LANES):
        lf2[p_me, :, lanes(k)] = to_lanes(jnp.sum(part[lanes(k), :], axis=1, keepdims=True))
    exchange(lf2, p_me, row_others, s_f2, r_f2)
    mass = tree(jnp.add, [lf2[i] for i in range(plan.gr)]) * float(plan.total)
    spread(1.0 / mass)
    f_line = f_line - jnp.log(mass)
    for i in range(plan.gr):
        f_own[i] = f_line[:, i * blk : (i + 1) * blk]
    for i in range(plan.gc):
        g_own[i] = g_line[:, i * blk : (i + 1) * blk]

    def last(r, carry):
        here = group(r)
        u_here = wide[here, :]
        mass_c, cost_c = carry
        new_mass, new_cost = [], []
        for c in range(n_parts):
            value = u_here * kern[here, lanes(c)]
            new_mass.append(mass_c[c] + value)
            new_cost.append(cost_c[c] + value * dist[here, lanes(c)])
        return tuple(new_mass), tuple(new_cost)

    mass_c, cost_c = lax.fori_loop(0, n_groups, last, (zeros, zeros), unroll=2)

    def finish(values):
        return jnp.concatenate(
            [
                jnp.sum(values[c] * scale[:, lanes(c)], axis=0, keepdims=True)
                for c in range(n_parts)
            ],
            axis=1,
        )

    both = jnp.concatenate([finish(mass_c), finish(cost_c)], axis=0)
    for i in range(plan.gc):
        cw_out[i] = both[:, i * blk : (i + 1) * blk]
    copies = [
        pltpu.make_async_remote_copy(
            src_ref=cw_out.at[other],
            dst_ref=cw_in.at[q_me],
            send_sem=s_c.at[i],
            recv_sem=r_c.at[q_me],
            device_id=device,
            device_id_type=MESH,
        )
        for i, (device, other) in enumerate(col_others)
    ]
    for copy in copies:
        copy.start()
    started.extend(copies)
    cw_in[q_me] = cw_out[q_me]
    for i, (device, other) in enumerate(col_others):
        pltpu.make_async_remote_copy(
            src_ref=cw_out.at[other],
            dst_ref=cw_in.at[other],
            send_sem=s_c.at[i],
            recv_sem=r_c.at[other],
            device_id=device,
            device_id_type=MESH,
        ).wait_recv()
    total = tree(jnp.add, [cw_in[i] for i in range(plan.gc)])
    fo_ref[...] = f_own[p_me]
    go_ref[...] = g_own[q_me] - jnp.log(total[0:1] * float(plan.total))
    ro_ref[...] = total[1:2] / total[0:1] * -EPS
    for copy in started:
        copy.wait_send()


def body(plan, demo, rollout):
    blk, width, rows, cols = plan.blk, plan.width, plan.rows, plan.cols
    n_dem = plan.pieces * ((plan.zl - 1) + (plan.x - 1) * plan.zl)
    n_rol = plan.pieces * (
        (plan.zh - 1) + (plan.y - 1) * plan.zh + plan.zh * plan.y
    )
    dma = pltpu.SemaphoreType.DMA
    f32 = jnp.float32
    outs = pl.pallas_call(
        functools.partial(kernel, plan),
        out_shape=[jax.ShapeDtypeStruct((1, blk), f32)] * 3,
        in_specs=[pl.BlockSpec(memory_space=pltpu.VMEM)] * 2,
        out_specs=[pl.BlockSpec(memory_space=pltpu.VMEM)] * 3,
        scratch_shapes=[
            pltpu.VMEM((rows, width), jnp.bfloat16),
            pltpu.VMEM((cols, width), jnp.bfloat16),
            pltpu.VMEM((rows, cols), f32),
            pltpu.VMEM((rows, cols), f32),
            pltpu.VMEM((rows, LANES), f32),
            pltpu.VMEM((rows, LANES), f32),
            pltpu.VMEM((rows, LANES), f32),
            pltpu.VMEM((SUB, cols), f32),
            pltpu.VMEM((plan.gr, 1, rows), f32),
            pltpu.VMEM((plan.gr, 1, rows), f32),
            pltpu.VMEM((plan.gc, 1, cols), f32),
            pltpu.VMEM((plan.gr, 1, blk), f32),
            pltpu.VMEM((plan.gc, 1, blk), f32),
            pltpu.VMEM((plan.gc, 2, blk), f32),
            pltpu.VMEM((plan.gc, 2, blk), f32),
            dma((n_dem,)),
            dma((plan.gr, plan.pieces)),
            dma((n_rol,)),
            dma((plan.gc, plan.pieces)),
            dma((plan.gr,)),
            dma((plan.gr,)),
            dma((plan.gr,)),
            dma((plan.gr,)),
            dma((plan.gc,)),
            dma((plan.gc,)),
            dma((plan.gc,)),
            dma((plan.gc,)),
        ],
        compiler_params=pltpu.CompilerParams(
            collective_id=0, has_side_effects=True, vmem_limit_bytes=48 * 1024 * 1024
        ),
    )(demo, rollout)
    return tuple(o.reshape(blk) for o in outs)


def solution(mesh):
    rows_axis, cols_axis = mesh.shape["row"], mesh.shape["col"]

    def run(demo, rollout):
        blk = demo.shape[0] // (rows_axis * cols_axis)
        plan = Plan(rows_axis, cols_axis, blk, demo.shape[1])
        return jax.shard_map(
            functools.partial(body, plan),
            mesh=mesh,
            in_specs=(P(("row", "col"), None), P(("row", "col"), None)),
            out_specs=(P(("row", "col")), P(("row", "col")), P(("row", "col"))),
            check_vma=False,
        )(demo, rollout)

    return run
```

time: 192 us -> 45.2 us (0.24)
  blocking collectives: 116 us -> 0 us
  other arithmetic: 43.2 us -> 0 us
  Pallas kernels: 0 us -> 40.9 us
  between operations: 14.2 us -> 0.65 us
  waiting for transfers between devices: 11.4 us -> 0 us
  matrix products: 5.75 us -> 0 us
  local copies, waits for them, and re-layouts: 0.63 us -> 3.49 us
    psum x5 -> x0, blocking collectives: 57.8 us -> none  [the longest x2 27.8 us: over_rows(): total = lax.psum(jnp.sum(jnp.exp(expo - top[None, :]), axis=0), 'row')]
    pmax x4 -> x0, blocking collectives: 46.5 us -> none  [the longest x2 27.8 us: over_rows(): top = lax.pmax(top, 'row')]
    pallas_call x0 -> x1, Pallas kernels: none -> 40.9 us  [body(): pl.pallas_call(functools.partial(kernel, plan), out_shape=[jax.ShapeDtype...]
    reduce_sum x7 -> x0, other arithmetic: 25.7 us -> none  [the longest x2 9.26 us: over_rows(): total = lax.psum(jnp.sum(jnp.exp(expo - top[None, :]), axis=0), 'row')]
    reduce_max x3 -> x0, other arithmetic: 13.6 us -> none  [the longest x2 9.07 us: over_rows(): top = jnp.max(expo, axis=0)]
    all_gather x1 -> x0, blocking collectives: 11.5 us -> none  [body(): demo_unit = lax.all_gather(normalize(demo), 'col', axis=0, tiled=True)]
    all_gather x1 -> x0, waiting for transfers between devices: 11.4 us -> none  [body(): rollout_unit = lax.all_gather(normalize(rollout), 'row', axis=0, tiled=True)]
    dot_general x1 -> x0, matrix products: 5.75 us -> none  [cost_of(): lax.dot_general(left, right, (((1,), (1,)), ((), ())), preferred_element_...]
  transfers between devices with their start and end apart: 1 -> 0, of which waited for: 1 -> 0; matrix products, arithmetic and copies ran while one was open for 1% -> 0% of each run, Pallas kernels for 0% -> 0%
where the time goes in v1:
time: 45.2 us; the launch traced here: 45.1 us
  Pallas kernels  40.9 us (90%)
  local copies, waits for them, and re-layouts  3.49 us (8%)
  between operations  0.65 us (1%)
    pallas_call x1, Pallas kernels, body(): pl.pallas_call(functools.partial(kernel, plan), out_shape=[jax.ShapeDtype...  40.9 us
    unnamed x7, local copies, waits for them, and re-layouts  3.49 us

profile of v1, /device:TPU:0, one launch (start us, length us, event | category | flops | bytes accessed | tf_op | source)
XLA Modules:
  0.0 45.1 jit_solution(6085998089878544145)
XLA Ops:
  0.6 0.0 copy-start
  0.6 0.9 %copy-done = bf16[256,256]{1,0:T(8,128)(2,1)S(1)} copy-done((bf16[256,256]{1,0:T(8,128)(2,1)S(1)}, bf16[256,256]{1,0:T(8,128)(2,1)}, u32[]{:S(2)}) %copy-start) | copy-done | bytes 131096
  1.5 0.0 copy-start.1
  1.5 0.9 %copy-done.1 = bf16[256,256]{1,0:T(8,128)(2,1)S(1)} copy-done((bf16[256,256]{1,0:T(8,128)(2,1)S(1)}, bf16[256,256]{1,0:T(8,128)(2,1)}, u32[]{:S(2)}) %copy-start.1) | copy-done | bytes 131096
  2.4 40.9 %shard_map.49 = (f32[1,256]{1,0:T(1,128)S(1)}, f32[1,256]{1,0:T(1,128)S(1)}, f32[1,256]{1,0:T(1,128)S(1)}) custom-call(bf16[256,256]{1,0:T(8,128)(2,1)S(1)} %copy-done, bf16[256,256]{1,0:T(8,128)(2,1)S(1)} %copy-done.1), custom_call_target="tpu_custom_call" | custom-call | tf_op jit(solution)/shard_map/pallas_call | solution.py:396
  43.4 0.6 %copy.8 = f32[256]{0:T(256)} copy(f32[256]{0:T(256)S(1)} %bitcast.5) | data formatting | bytes 2048
  44.0 0.6 %copy.9 = f32[256]{0:T(256)} copy(f32[256]{0:T(256)S(1)} %bitcast.4) | data formatting | bytes 2048
  44.5 0.6 %copy.10 = f32[256]{0:T(256)} copy(f32[256]{0:T(256)S(1)} %bitcast.3) | data formatting | bytes 2048
Async XLA Ops:
  0.6 0.9 %copy-start = (bf16[256,256]{1,0:T(8,128)(2,1)S(1)}, bf16[256,256]{1,0:T(8,128)(2,1)}, u32[]{:S(2)}) copy-start(bf16[256,256]{1,0:T(8,128)(2,1)} %demo_ref.1) | copy-start | bytes 393220
  1.5 0.9 %copy-start.1 = (bf16[256,256]{1,0:T(8,128)(2,1)S(1)}, bf16[256,256]{1,0:T(8,128)(2,1)}, u32[]{:S(2)}) copy-start(bf16[256,256]{1,0:T(8,128)(2,1)} %roll_ref.1) | copy-start | bytes 393220

commit v2 on v1

v2 whole, which is shorter than its diff:
```python
import functools
import math

import jax
import jax.numpy as jnp
from jax import lax
from jax.experimental import pallas as pl
from jax.experimental.pallas import tpu as pltpu
from jax.sharding import PartitionSpec as P

EPS = 0.005
MESH = pl.DeviceIdType.MESH
LANES = 128
SUB = 8


class Plan:
    def __init__(self, rows_axis, cols_axis, blk, width):
        self.core = 2
        depth = rows_axis // 2
        self.x = 1 << ((cols_axis.bit_length() - 1) // 2)
        self.y = cols_axis // self.x
        self.zl = min(depth, max(1, cols_axis // self.x))
        self.zh = depth // self.zl
        self.blk = blk
        self.width = width
        self.gr = self.zl * self.x
        self.gc = self.zh * self.y * self.core
        self.rows = self.gr * blk
        self.cols = self.gc * blk
        self.total = rows_axis * cols_axis * blk
        self.pieces = max(1, min(4, blk // 16))
        self.piece = blk // self.pieces
        self.chunks = 4 if blk % LANES == 0 and self.gr % 4 == 0 else 1


def normalize(embed):
    values = embed.astype(jnp.float32)
    inverse = lax.rsqrt(jnp.sum(values * values, axis=-1, keepdims=True) + 1e-06)
    return (values * inverse).astype(jnp.bfloat16)


def tree(op, items):
    items = list(items)
    while len(items) > 1:
        items = [
            op(items[i], items[i + 1]) if i + 1 < len(items) else items[i]
            for i in range(0, len(items), 2)
        ]
    return items[0]


def kernel(
    plan,
    demo_hbm,
    roll_hbm,
    out_ref,
    demo_ref,
    roll_ref,
    dem,
    rol,
    dist,
    kern,
    best,
    part,
    wide,
    scale,
    lf1,
    lf2,
    lg,
    f_all,
    g_all,
    cw_out,
    cw_in,
    s_in,
    s_dem,
    r_dem,
    s_rol,
    r_rol,
    s_f1,
    r_f1,
    s_f2,
    r_f2,
    s_g,
    r_g,
    s_c,
    r_c,
):
    blk, rows, cols = plan.blk, plan.rows, plan.cols
    n_parts = cols // LANES
    chunks, chunk = plan.chunks, rows // plan.chunks
    row = lax.axis_index("row")
    col = lax.axis_index("col")
    core, z = lax.rem(row, 2), row // 2
    zlo, zhi = lax.rem(z, plan.zl), z // plan.zl
    x, y = lax.rem(col, plan.x), col // plan.x

    load_demo = pltpu.make_async_copy(demo_hbm, demo_ref, s_in.at[0])
    load_roll = pltpu.make_async_copy(roll_hbm, roll_ref, s_in.at[1])
    load_demo.start()
    load_roll.start()

    def row_peer(dz, dx):
        zz, xx = lax.rem(zlo + dz, plan.zl), lax.rem(x + dx, plan.x)
        device = ((zhi * plan.zl + zz) * 2 + core, y * plan.x + xx)
        return device, zz * plan.x + xx

    def col_peer(dz, dy, dc):
        zz, yy, cc = lax.rem(zhi + dz, plan.zh), lax.rem(y + dy, plan.y), lax.rem(core + dc, 2)
        device = ((zz * plan.zl + zlo) * 2 + cc, yy * plan.x + x)
        return device, (zz * plan.y + yy) * 2 + cc

    row_offsets = [(a, b) for a in range(plan.zl) for b in range(plan.x)]
    col_offsets = [(a, b, c) for a in range(plan.zh) for b in range(plan.y) for c in range(2)]
    row_peers = {o: row_peer(*o) for o in row_offsets}
    col_peers = {o: col_peer(*o) for o in col_offsets}
    p_me = row_peers[(0, 0)][1]
    q_me = col_peers[(0, 0, 0)][1]
    row_others = [row_peers[o] for o in row_offsets[1:]]
    col_others = [col_peers[o] for o in col_offsets[1:]]
    places = [col_peers[o][1] for o in col_offsets]

    barrier = pltpu.get_barrier_semaphore()
    for device, _ in row_others + col_others:
        pl.semaphore_signal(barrier, inc=1, device_id=device, device_id_type=MESH)

    def slot(buf, index, piece):
        start = pl.multiple_of(index * blk + piece * plan.piece, 16)
        return buf.at[pl.ds(start, plan.piece), :]

    load_demo.wait()
    dem[pl.ds(pl.multiple_of(p_me * blk, 16), blk), :] = normalize(demo_ref[...])
    load_roll.wait()
    rol[pl.ds(pl.multiple_of(q_me * blk, 16), blk), :] = normalize(roll_ref[...])
    pl.semaphore_wait(barrier, len(row_others) + len(col_others))

    partner = col_peers[(0, 0, 1)][0]
    started = []

    def send(buf, index, piece, device, ssem, rsem, count):
        ref = slot(buf, index, piece)
        copy = pltpu.make_async_remote_copy(
            src_ref=ref,
            dst_ref=ref,
            send_sem=ssem.at[count[0]],
            recv_sem=rsem.at[index, piece],
            device_id=device,
            device_id_type=MESH,
        )
        copy.start()
        count[0] += 1
        started.append(copy)

    def arrived(buf, index, piece, ssem, rsem):
        ref = slot(buf, index, piece)
        pltpu.make_async_remote_copy(
            src_ref=ref,
            dst_ref=ref,
            send_sem=ssem.at[0],
            recv_sem=rsem.at[index, piece],
            device_id=partner,
            device_id_type=MESH,
        ).wait_recv()

    n_dem, n_rol = [0], [0]
    send_dem = lambda i, k, d: send(dem, i, k, d, s_dem, r_dem, n_dem)
    send_rol = lambda i, k, d: send(rol, i, k, d, s_rol, r_rol, n_rol)
    for k in range(plan.pieces):
        for dz in range(1, plan.zl):
            send_dem(p_me, k, row_peers[(dz, 0)][0])
        for dz in range(1, plan.zh):
            send_rol(q_me, k, col_peers[(dz, 0, 0)][0])
        for dx in range(1, plan.x):
            send_dem(p_me, k, row_peers[(0, dx)][0])
        for dy in range(1, plan.y):
            send_rol(q_me, k, col_peers[(0, dy, 0)][0])
        send_rol(q_me, k, partner)
    for k in range(plan.pieces):
        for dz in range(1, plan.zl):
            index = row_peers[(dz, 0)][1]
            arrived(dem, index, k, s_dem, r_dem)
            for dx in range(1, plan.x):
                send_dem(index, k, row_peers[(0, dx)][0])
        for dz in range(1, plan.zh):
            index = col_peers[(dz, 0, 0)][1]
            arrived(rol, index, k, s_rol, r_rol)
            for dy in range(1, plan.y):
                send_rol(index, k, col_peers[(0, dy, 0)][0])
            send_rol(index, k, partner)
        for dy in range(1, plan.y):
            index = col_peers[(0, dy, 0)][1]
            arrived(rol, index, k, s_rol, r_rol)
            send_rol(index, k, partner)
    for k in range(plan.pieces):
        for dz in range(plan.zl):
            for dx in range(1, plan.x):
                arrived(dem, row_peers[(dz, dx)][1], k, s_dem, r_dem)

    def lanes(c):
        return slice(c * LANES, (c + 1) * LANES)

    def group(r):
        return pl.ds(pl.multiple_of(r * SUB, SUB), SUB)

    def over(h, body, init, unroll):
        first = h * chunk // SUB
        return lax.fori_loop(first, first + chunk // SUB, body, init, unroll=unroll)

    eye = lax.broadcasted_iota(jnp.int32, (LANES, LANES), 0) == lax.broadcasted_iota(
        jnp.int32, (LANES, LANES), 1
    )

    def to_lanes(column):
        return jnp.sum(jnp.where(eye, column, 0.0), axis=0, keepdims=True)

    def tile(where, count):
        for i in range(where, where + count):
            inner = lax.dot_general(
                dem[...],
                rol[pl.ds(pl.multiple_of(places[i] * blk, 16), blk), :],
                (((1,), (1,)), ((), ())),
                preferred_element_type=jnp.float32,
            )
            dist[:, i * blk : (i + 1) * blk] = (1.0 - inner) * (1.0 / EPS)

    def row_stats(h, first, count, fresh):
        def step(r, carry):
            here = group(r)
            values = [dist[here, lanes(c)] for c in range(first, first + count)]
            low = tree(jnp.minimum, values)
            if not fresh:
                before = best[here, :]
                low = jnp.minimum(low, before)
            total = tree(jnp.add, [jnp.exp(low - v) for v in values])
            if not fresh:
                total = total + part[here, :] * jnp.exp(low - before)
            best[here, :] = low
            part[here, :] = total
            return carry

        over(h, step, 0, 4)

    def store_line(buf, index, k, line):
        at = k * LANES
        done = 0
        while done < LANES:
            i, j = (at + done) // blk, (at + done) % blk
            n = min(LANES - done, blk - j)
            buf[index, i : i + 1, j : j + n] = line[:, done : done + n]
            done += n

    def exchange_start(buf, index, others, ssem, rsem, h, slots):
        here = pl.ds(h * slots, slots)
        for i, (device, _) in enumerate(others):
            copy = pltpu.make_async_remote_copy(
                src_ref=buf.at[index, here],
                dst_ref=buf.at[index, here],
                send_sem=ssem.at[i, h],
                recv_sem=rsem.at[index, h],
                device_id=device,
                device_id_type=MESH,
            )
            copy.start()
            started.append(copy)

    def exchange_wait(buf, others, ssem, rsem, h, slots):
        here = pl.ds(h * slots, slots)
        for i, (device, other) in enumerate(others):
            pltpu.make_async_remote_copy(
                src_ref=buf.at[other, here],
                dst_ref=buf.at[other, here],
                send_sem=ssem.at[i, h],
                recv_sem=rsem.at[other, h],
                device_id=device,
                device_id_type=MESH,
            ).wait_recv()

    def log_total(values):
        top = tree(jnp.maximum, values)
        return top + jnp.log(tree(jnp.add, [jnp.exp(v - top) for v in values]))

    def line_of(pieces):
        return pieces[0] if len(pieces) == 1 else jnp.concatenate(pieces, axis=1)

    def spread(h, values):
        line = line_of([values[i : i + 1, :] for i in range(values.shape[0])])
        for k in range(chunk // LANES):
            column = jnp.sum(jnp.where(eye, line[:, lanes(k)], 0.0), axis=1, keepdims=True)
            wide[lanes(h * (chunk // LANES) + k), :] = jnp.broadcast_to(column, (LANES, LANES))

    per_chunk = chunk // LANES
    slots = chunk // blk
    log_n = math.log(plan.total)

    every = [o for o in col_offsets if o[2] == 0]
    fresh = True
    done = 0
    for at, (dz, dy, _) in enumerate(every):
        if dz > 0 and dy > 0:
            for k in range(plan.pieces):
                index = col_peers[(dz, dy, 0)][1]
                arrived(rol, index, k, s_rol, r_rol)
                send_rol(index, k, partner)
        for k in range(plan.pieces):
            arrived(rol, col_peers[(dz, dy, 1)][1], k, s_rol, r_rol)
        tile(2 * at, 2)
        if (2 * (at + 1) * blk) % LANES == 0 and at + 1 < len(every):
            upto = 2 * (at + 1) * blk // LANES
            for h in range(chunks):
                row_stats(h, done, upto - done, fresh)
            fresh, done = False, upto
    for h in range(chunks):
        row_stats(h, done, n_parts - done, fresh)
        for k in range(h * per_chunk, (h + 1) * per_chunk):
            low = best[lanes(k), :]
            least = jnp.min(low, axis=1, keepdims=True)
            total = jnp.sum(part[lanes(k), :] * jnp.exp(least - low), axis=1, keepdims=True)
            store_line(lf1, p_me, k, jnp.log(to_lanes(total)) - to_lanes(least))
        exchange_start(lf1, p_me, row_others, s_f1, r_f1, h, slots)

    def col_max(r, carry):
        here = group(r)
        f_here = wide[here, :]
        return tuple(
            jnp.maximum(carry[c], f_here - dist[here, lanes(c)]) for c in range(n_parts)
        )

    tops = tuple(jnp.full((SUB, LANES), -jnp.inf, jnp.float32) for _ in range(n_parts))
    for h in range(chunks):
        exchange_wait(lf1, row_others, s_f1, r_f1, h, slots)
        here = pl.ds(h * slots, slots)
        f_all[here, :] = -log_n - log_total([lf1[i, here, :] for i in range(plan.gr)])
        spread(h, f_all[here, :])
        tops = over(h, col_max, tops, 4)

    def col_sum(r, carry):
        here = group(r)
        f_here = wide[here, :]
        out = []
        for c in range(n_parts):
            value = jnp.exp((f_here - dist[here, lanes(c)]) - tops[c])
            kern[here, lanes(c)] = value
            out.append(carry[c] + value)
        return tuple(out)

    zeros = tuple(jnp.zeros((SUB, LANES), jnp.float32) for _ in range(n_parts))
    sums = lax.fori_loop(0, rows // SUB, col_sum, zeros, unroll=4)
    pieces = []
    for c in range(n_parts):
        top = jnp.max(tops[c], axis=0, keepdims=True)
        total = jnp.sum(sums[c] * jnp.exp(tops[c] - top), axis=0, keepdims=True)
        pieces.append(top + jnp.log(total))
    line = line_of(pieces)
    for i, place in enumerate(places):
        lg[q_me, pl.ds(place, 1), :] = line[:, i * blk : (i + 1) * blk]
    exchange_start(lg, q_me, col_others, s_g, r_g, 0, plan.gc)
    exchange_wait(lg, col_others, s_g, r_g, 0, plan.gc)
    g_all[...] = -log_n - log_total([lg[i] for i in range(plan.gc)])
    g_line = line_of([g_all[pl.ds(place, 1), :] for place in places])
    for c in range(n_parts):
        scale[:, lanes(c)] = jnp.exp(tops[c] + g_line[:, lanes(c)])

    def second_rows(r, carry):
        here = group(r)
        part[here, :] = tree(
            jnp.add, [kern[here, lanes(c)] * scale[:, lanes(c)] for c in range(n_parts)]
        )
        return carry

    for h in range(chunks):
        over(h, second_rows, 0, 4)
        for k in range(h * per_chunk, (h + 1) * per_chunk):
            total = jnp.sum(part[lanes(k), :], axis=1, keepdims=True)
            store_line(lf2, p_me, k, to_lanes(total))
        exchange_start(lf2, p_me, row_others, s_f2, r_f2, h, slots)

    def last(r, carry):
        here = group(r)
        u_here = wide[here, :]
        mass_c, cost_c = carry
        new_mass, new_cost = [], []
        for c in range(n_parts):
            value = u_here * kern[here, lanes(c)]
            new_mass.append(mass_c[c] + value)
            new_cost.append(cost_c[c] + value * dist[here, lanes(c)])
        return tuple(new_mass), tuple(new_cost)

    both = (zeros, zeros)
    for h in range(chunks):
        exchange_wait(lf2, row_others, s_f2, r_f2, h, slots)
        here = pl.ds(h * slots, slots)
        mass = tree(jnp.add, [lf2[i, here, :] for i in range(plan.gr)]) * float(plan.total)
        spread(h, 1.0 / mass)
        f_all[here, :] = f_all[here, :] - jnp.log(mass)
        both = over(h, last, both, 2)

    def finish(values):
        return line_of(
            [
                jnp.sum(values[c] * scale[:, lanes(c)], axis=0, keepdims=True)
                for c in range(n_parts)
            ]
        )

    both = jnp.concatenate([finish(both[0]), finish(both[1])], axis=0)
    for i, place in enumerate(places):
        cw_out[place] = both[:, i * blk : (i + 1) * blk]
    for i, (device, other) in enumerate(col_others):
        copy = pltpu.make_async_remote_copy(
            src_ref=cw_out.at[other],
            dst_ref=cw_in.at[q_me],
            send_sem=s_c.at[i],
            recv_sem=r_c.at[q_me],
            device_id=device,
            device_id_type=MESH,
        )
        copy.start()
        started.append(copy)
    cw_in[q_me] = cw_out[q_me]
    for i, (device, other) in enumerate(col_others):
        pltpu.make_async_remote_copy(
            src_ref=cw_out.at[other],
            dst_ref=cw_in.at[other],
            send_sem=s_c.at[i],
            recv_sem=r_c.at[other],
            device_id=device,
            device_id_type=MESH,
        ).wait_recv()
    total = tree(jnp.add, [cw_in[i] for i in range(plan.gc)])
    out_ref[0:1, :] = f_all[pl.ds(p_me, 1), :]
    out_ref[1:2, :] = g_all[pl.ds(q_me, 1), :] - jnp.log(total[0:1] * float(plan.total))
    out_ref[2:3, :] = total[1:2] / total[0:1] * -EPS
    for copy in started:
        copy.wait_send()


def body(plan, demo, rollout):
    blk, width, rows, cols = plan.blk, plan.width, plan.rows, plan.cols
    n_dem = plan.pieces * ((plan.zl - 1) + (plan.x - 1) * plan.zl)
    n_rol = plan.pieces * (
        (plan.zh - 1) + (plan.y - 1) * plan.zh + plan.zh * plan.y
    )
    dma = pltpu.SemaphoreType.DMA
    f32 = jnp.float32
    out = pl.pallas_call(
        functools.partial(kernel, plan),
        out_shape=jax.ShapeDtypeStruct((3, blk), f32),
        in_specs=[pl.BlockSpec(memory_space=pltpu.HBM)] * 2,
        out_specs=pl.BlockSpec(memory_space=pltpu.VMEM),
        scratch_shapes=[
            pltpu.VMEM((blk, width), jnp.bfloat16),
            pltpu.VMEM((blk, width), jnp.bfloat16),
            pltpu.VMEM((rows, width), jnp.bfloat16),
            pltpu.VMEM((cols, width), jnp.bfloat16),
            pltpu.VMEM((rows, cols), f32),
            pltpu.VMEM((rows, cols), f32),
            pltpu.VMEM((rows, LANES), f32),
            pltpu.VMEM((rows, LANES), f32),
            pltpu.VMEM((rows, LANES), f32),
            pltpu.VMEM((SUB, cols), f32),
            pltpu.VMEM((plan.gr, plan.gr, blk), f32),
            pltpu.VMEM((plan.gr, plan.gr, blk), f32),
            pltpu.VMEM((plan.gc, plan.gc, blk), f32),
            pltpu.VMEM((plan.gr, blk), f32),
            pltpu.VMEM((plan.gc, blk), f32),
            pltpu.VMEM((plan.gc, 2, blk), f32),
            pltpu.VMEM((plan.gc, 2, blk), f32),
            dma((2,)),
            dma((n_dem,)),
            dma((plan.gr, plan.pieces)),
            dma((n_rol,)),
            dma((plan.gc, plan.pieces)),
            dma((plan.gr, plan.chunks)),
            dma((plan.gr, plan.chunks)),
            dma((plan.gr, plan.chunks)),
            dma((plan.gr, plan.chunks)),
            dma((plan.gc, 1)),
            dma((plan.gc, 1)),
            dma((plan.gc,)),
            dma((plan.gc,)),
        ],
        compiler_params=pltpu.CompilerParams(
            collective_id=0, has_side_effects=True, vmem_limit_bytes=48 * 1024 * 1024
        ),
    )(demo, rollout)
    return out[0], out[1], out[2]


def solution(mesh):
    rows_axis, cols_axis = mesh.shape["row"], mesh.shape["col"]

    def run(demo, rollout):
        blk = demo.shape[0] // (rows_axis * cols_axis)
        plan = Plan(rows_axis, cols_axis, blk, demo.shape[1])
        return jax.shard_map(
            functools.partial(body, plan),
            mesh=mesh,
            in_specs=(P(("row", "col"), None), P(("row", "col"), None)),
            out_specs=(P(("row", "col")), P(("row", "col")), P(("row", "col"))),
            check_vma=False,
        )(demo, rollout)

    return run
```

time: 45.2 us -> 46.5 us (1.029)
  Pallas kernels: 40.9 us -> 43.4 us
  local copies, waits for them, and re-layouts: 3.49 us -> 2.38 us
    pallas_call x1, Pallas kernels: 40.9 us -> 43.4 us  [body(): pl.pallas_call(functools.partial(kernel, plan), out_shape=jax.ShapeDtypeS...]
    unnamed x7 -> x4, local copies, waits for them, and re-layouts: 3.49 us -> 1.8 us
    slice x0 -> x1, local copies, waits for them, and re-layouts: none -> 0.57 us  [body(): return (out[0], out[1], out[2])]
where the time goes in v2:
time: 46.5 us; the launch traced here: 46.4 us
  Pallas kernels  43.4 us (93%)
  local copies, waits for them, and re-layouts  2.38 us (5%)
  between operations  0.65 us (1%)
    pallas_call x1, Pallas kernels, body(): pl.pallas_call(functools.partial(kernel, plan), out_shape=jax.ShapeDtypeS...  43.4 us
    unnamed x4, local copies, waits for them, and re-layouts  1.8 us

profile of v2, /device:TPU:0, one launch (start us, length us, event | category | flops | bytes accessed | tf_op | source)
XLA Modules:
  0.0 46.4 jit_solution(11282242171295767273)
XLA Ops:
  0.6 0.0 copy-start
  0.6 0.9 %copy-done = bf16[256,256]{1,0:T(8,128)(2,1)S(1)} copy-done((bf16[256,256]{1,0:T(8,128)(2,1)S(1)}, bf16[256,256]{1,0:T(8,128)(2,1)}, u32[]{:S(2)}) %copy-start) | copy-done | bytes 131096
  1.5 0.0 copy-start.1
  1.5 0.9 %copy-done.1 = bf16[256,256]{1,0:T(8,128)(2,1)S(1)} copy-done((bf16[256,256]{1,0:T(8,128)(2,1)S(1)}, bf16[256,256]{1,0:T(8,128)(2,1)}, u32[]{:S(2)}) %copy-start.1) | copy-done | bytes 131096
  2.4 43.4 %shard_map.49 = f32[3,256]{1,0:T(4,128)S(1)} custom-call(bf16[256,256]{1,0:T(8,128)(2,1)S(1)} %copy-done, bf16[256,256]{1,0:T(8,128)(2,1)S(1)} %copy-done.1), custom_call_target="tpu_custom_call" | custom-call | tf_op jit(solution)/shard_map/pallas_call | solution.py:445
  45.8 0.6 %fusion = (f32[1,256]{1,0:T(1,128)}, f32[1,256]{1,0:T(1,128)}, f32[1,256]{1,0:T(1,128)}) fusion(f32[3,256]{1,0:T(4,128)S(1)} %shard_map.49), kind=kLoop, calls=%fused_computation | loop fusion | bytes 6144 | tf_op jit(solution)/shard_map/slice | solution.py:486
Async XLA Ops:
  0.6 0.9 %copy-start = (bf16[256,256]{1,0:T(8,128)(2,1)S(1)}, bf16[256,256]{1,0:T(8,128)(2,1)}, u32[]{:S(2)}) copy-start(bf16[256,256]{1,0:T(8,128)(2,1)} %demo_hbm.1) | copy-start | bytes 393220
  1.5 0.9 %copy-start.1 = (bf16[256,256]{1,0:T(8,128)(2,1)S(1)}, bf16[256,256]{1,0:T(8,128)(2,1)}, u32[]{:S(2)}) copy-start(bf16[256,256]{1,0:T(8,128)(2,1)} %roll_hbm.1) | copy-start | bytes 393220

commit v3 on v2

--- a/solution.py
+++ b/solution.py
@@ -31,7 +31,7 @@
         self.total = rows_axis * cols_axis * blk
         self.pieces = max(1, min(4, blk // 16))
         self.piece = blk // self.pieces
-        self.chunks = 4 if blk % LANES == 0 and self.gr % 4 == 0 else 1
+        self.chunks = 2 if blk % LANES == 0 and self.gr % 2 == 0 else 1
 
 
 def normalize(embed):
@@ -238,7 +238,7 @@
             part[here, :] = total
             return carry
 
-        over(h, step, 0, 4)
+        over(h, step, 0, max(4, 64 // count))
 
     def store_line(buf, index, k, line):
         at = k * LANES
@@ -331,7 +331,7 @@
         here = pl.ds(h * slots, slots)
         f_all[here, :] = -log_n - log_total([lf1[i, here, :] for i in range(plan.gr)])
         spread(h, f_all[here, :])
-        tops = over(h, col_max, tops, 4)
+        tops = over(h, col_max, tops, 8)
 
     def col_sum(r, carry):
         here = group(r)
@@ -344,7 +344,7 @@
         return tuple(out)
 
     zeros = tuple(jnp.zeros((SUB, LANES), jnp.float32) for _ in range(n_parts))
-    sums = lax.fori_loop(0, rows // SUB, col_sum, zeros, unroll=4)
+    sums = lax.fori_loop(0, rows // SUB, col_sum, zeros, unroll=8)
     pieces = []
     for c in range(n_parts):
         top = jnp.max(tops[c], axis=0, keepdims=True)
@@ -368,7 +368,7 @@
         return carry
 
     for h in range(chunks):
-        over(h, second_rows, 0, 4)
+        over(h, second_rows, 0, 8)
         for k in range(h * per_chunk, (h + 1) * per_chunk):
             total = jnp.sum(part[lanes(k), :], axis=1, keepdims=True)
             store_line(lf2, p_me, k, to_lanes(total))
@@ -392,7 +392,7 @@
         mass = tree(jnp.add, [lf2[i, here, :] for i in range(plan.gr)]) * float(plan.total)
         spread(h, 1.0 / mass)
         f_all[here, :] = f_all[here, :] - jnp.log(mass)
-        both = over(h, last, both, 2)
+        both = over(h, last, both, 4)
 
     def finish(values):
         return line_of(
@@ -480,7 +480,7 @@
             dma((plan.gc,)),
         ],
         compiler_params=pltpu.CompilerParams(
-            collective_id=0, has_side_effects=True, vmem_limit_bytes=48 * 1024 * 1024
+            collective_id=0, has_side_effects=True, vmem_limit_bytes=64 * 1024 * 1024 - 128 * 1024
         ),
     )(demo, rollout)
     return out[0], out[1], out[2]

time: 46.5 us -> 43.6 us (0.938)
  Pallas kernels: 43.4 us -> 41.5 us
  local copies, waits for them, and re-layouts: 2.38 us -> 1.36 us
    pallas_call x1, Pallas kernels: 43.4 us -> 41.5 us  [body(): pl.pallas_call(functools.partial(kernel, plan), out_shape=jax.ShapeDtypeS...]
    unnamed x4 -> x0, local copies, waits for them, and re-layouts: 1.8 us -> none
    slice x1, local copies, waits for them, and re-layouts: 0.57 us -> 1.36 us  [body(): return (out[0], out[1], out[2])]
where the time goes in v3:
time: 43.6 us; the launch traced here: 43.5 us
  Pallas kernels  41.5 us (95%)
  local copies, waits for them, and re-layouts  1.36 us (3%)
  between operations  0.64 us (1%)
    pallas_call x1, Pallas kernels, body(): pl.pallas_call(functools.partial(kernel, plan), out_shape=jax.ShapeDtypeS...  41.5 us
    slice x1, local copies, waits for them, and re-layouts, body(): return (out[0], out[1], out[2])  1.36 us

profile of v3, /device:TPU:0, one launch (start us, length us, event | category | flops | bytes accessed | tf_op | source)
XLA Modules:
  0.0 43.5 jit_solution(1550262851326716021)
XLA Ops:
  0.6 41.5 %shard_map.49 = f32[3,256]{1,0:T(4,128)} custom-call(bf16[256,256]{1,0:T(8,128)(2,1)} %demo_hbm.1, bf16[256,256]{1,0:T(8,128)(2,1)} %roll_hbm.1), custom_call_target="tpu_custom_call" | custom-call | tf_op jit(solution)/shard_map/pallas_call | solution.py:445
  42.1 1.4 %fusion = (f32[1,256]{1,0:T(1,128)}, f32[1,256]{1,0:T(1,128)}, f32[1,256]{1,0:T(1,128)}) fusion(f32[3,256]{1,0:T(4,128)} %shard_map.49), kind=kLoop, calls=%fused_computation | loop fusion | bytes 6144 | tf_op jit(solution)/shard_map/slice | solution.py:486

commit v4 on v3

--- a/solution.py
+++ b/solution.py
@@ -12,6 +12,8 @@
 MESH = pl.DeviceIdType.MESH
 LANES = 128
 SUB = 8
+GROUPS = 8
+BLOCK = SUB * GROUPS
 
 
 class Plan:
@@ -31,6 +33,7 @@
         self.total = rows_axis * cols_axis * blk
         self.pieces = max(1, min(4, blk // 16))
         self.piece = blk // self.pieces
+        self.fine = blk % LANES == 0 and (self.zl, self.x, self.zh, self.y, self.pieces) == (2, 2, 2, 2, 4)
         self.chunks = 2 if blk % LANES == 0 and self.gr % 2 == 0 else 1
 
 
@@ -64,7 +67,10 @@
     best,
     part,
     wide,
-    scale,
+    tops,
+    sums,
+    mass_c,
+    cost_c,
     lf1,
     lf2,
     lg,
@@ -175,7 +181,111 @@
         for dy in range(1, plan.y):
             send_rol(q_me, k, col_peers[(0, dy, 0)][0])
         send_rol(q_me, k, partner)
-    for k in range(plan.pieces):
+    def lanes(c):
+        return slice(c * LANES, (c + 1) * LANES)
+
+    def group(r):
+        return pl.ds(pl.multiple_of(r * SUB, SUB), SUB)
+
+    def over(h, body, init, unroll):
+        first = h * chunk // BLOCK
+        return lax.fori_loop(first, first + chunk // BLOCK, body, init, unroll=unroll)
+
+    eye = lax.broadcasted_iota(jnp.int32, (LANES, LANES), 0) == lax.broadcasted_iota(
+        jnp.int32, (LANES, LANES), 1
+    )
+
+    def to_lanes(column):
+        return jnp.sum(jnp.where(eye, column, 0.0), axis=0, keepdims=True)
+
+    def tile(where, place):
+        first = 0 if where is None else pl.multiple_of(where * blk, 16)
+        here = pl.ds(first, rows if where is None else blk)
+        for i in range(2 * place, 2 * place + 2):
+            inner = lax.dot_general(
+                dem[here, :],
+                rol[pl.ds(pl.multiple_of(places[i] * blk, 16), blk), :],
+                (((1,), (1,)), ((), ())),
+                preferred_element_type=jnp.float32,
+            )
+            dist[here, i * blk : (i + 1) * blk] = (1.0 - inner) * (1.0 / EPS)
+
+    def row_stats(first_row, size, place):
+        pair = 2 * blk // LANES
+
+        def step(r, carry):
+            here = pl.ds(pl.multiple_of(first_row + r * SUB, SUB), SUB)
+            values = [dist[here, lanes(c)] for c in range(place * pair, (place + 1) * pair)]
+            low = tree(jnp.minimum, values)
+            if place > 0:
+                before = best[here, :]
+                low = jnp.minimum(low, before)
+            total = tree(jnp.add, [jnp.exp(low - v) for v in values])
+            if place > 0:
+                total = total + part[here, :] * jnp.exp(low - before)
+            best[here, :] = low
+            part[here, :] = total
+            return carry
+
+        lax.fori_loop(0, size // SUB, step, 0, unroll=16)
+
+    def unit(where, place):
+        tile(where, place)
+        row_stats(pl.multiple_of(where * blk, SUB), blk, place)
+
+    def store_line(buf, index, k, line):
+        at = k * LANES
+        done = 0
+        while done < LANES:
+            i, j = (at + done) // blk, (at + done) % blk
+            n = min(LANES - done, blk - j)
+            buf[index, i : i + 1, j : j + n] = line[:, done : done + n]
+            done += n
+
+    def exchange_start(buf, index, others, ssem, rsem, h, slots):
+        here = pl.ds(h * slots, slots)
+        for i, (device, _) in enumerate(others):
+            copy = pltpu.make_async_remote_copy(
+                src_ref=buf.at[index, here],
+                dst_ref=buf.at[index, here],
+                send_sem=ssem.at[i, h],
+                recv_sem=rsem.at[index, h],
+                device_id=device,
+                device_id_type=MESH,
+            )
+            copy.start()
+            started.append(copy)
+
+    def exchange_wait(buf, others, ssem, rsem, h, slots):
+        here = pl.ds(h * slots, slots)
+        for i, (device, other) in enumerate(others):
+            pltpu.make_async_remote_copy(
+                src_ref=buf.at[other, here],
+                dst_ref=buf.at[other, here],
+                send_sem=ssem.at[i, h],
+                recv_sem=rsem.at[other, h],
+                device_id=device,
+                device_id_type=MESH,
+            ).wait_recv()
+
+    def log_total(values):
+        top = tree(jnp.maximum, values)
+        return top + jnp.log(tree(jnp.add, [jnp.exp(v - top) for v in values]))
+
+    def line_of(pieces):
+        return pieces[0] if len(pieces) == 1 else jnp.concatenate(pieces, axis=1)
+
+    def spread(h, values):
+        line = line_of([values[i : i + 1, :] for i in range(values.shape[0])])
+        for k in range(chunk // LANES):
+            column = jnp.sum(jnp.where(eye, line[:, lanes(k)], 0.0), axis=1, keepdims=True)
+            wide[lanes(h * (chunk // LANES) + k), :] = jnp.broadcast_to(column, (LANES, LANES))
+
+    per_chunk = chunk // LANES
+    slots = chunk // blk
+    log_n = math.log(plan.total)
+
+    def forward(k):
         for dz in range(1, plan.zl):
             index = row_peers[(dz, 0)][1]
             arrived(dem, index, k, s_dem, r_dem)
@@ -191,126 +301,67 @@
             index = col_peers[(0, dy, 0)][1]
             arrived(rol, index, k, s_rol, r_rol)
             send_rol(index, k, partner)
-    for k in range(plan.pieces):
+
+    def relay():
+        for k in range(plan.pieces):
+            for dz in range(1, plan.zh):
+                for dy in range(1, plan.y):
+                    index = col_peers[(dz, dy, 0)][1]
+                    arrived(rol, index, k, s_rol, r_rol)
+                    send_rol(index, k, partner)
+
+    def rows_in(dz, dx):
+        index = row_peers[(dz, dx)][1]
+        for k in range(plan.pieces):
+            arrived(dem, index, k, s_dem, r_dem)
+        return index
+
+    def cols_in(dz, dy):
+        for k in range(plan.pieces):
+            arrived(rol, col_peers[(dz, dy, 1)][1], k, s_rol, r_rol)
+
+    if plan.fine:
+        own, near_y, near_z, far = range(4)
+        cols_in(0, 0)
+        unit(p_me, own)
+        forward(0)
+        forward(1)
+        row_x = rows_in(0, 1)
+        unit(row_x, own)
+        forward(2)
+        forward(3)
+        row_z = row_peers[(1, 0)][1]
+        cols_in(0, 1)
+        unit(p_me, near_y)
+        unit(row_z, own)
+        relay()
+        unit(row_x, near_y)
+        unit(row_z, near_y)
+        cols_in(1, 0)
+        for index in (p_me, row_x, row_z):
+            unit(index, near_z)
+        row_f = rows_in(1, 1)
+        for place in (own, near_y, near_z):
+            unit(row_f, place)
+        cols_in(1, 1)
+        tile(None, far)
+        last_place = far
+    else:
+        for k in range(plan.pieces):
+            forward(k)
+        relay()
         for dz in range(plan.zl):
             for dx in range(1, plan.x):
-                arrived(dem, row_peers[(dz, dx)][1], k, s_dem, r_dem)
-
-    def lanes(c):
-        return slice(c * LANES, (c + 1) * LANES)
-
-    def group(r):
-        return pl.ds(pl.multiple_of(r * SUB, SUB), SUB)
-
-    def over(h, body, init, unroll):
-        first = h * chunk // SUB
-        return lax.fori_loop(first, first + chunk // SUB, body, init, unroll=unroll)
-
-    eye = lax.broadcasted_iota(jnp.int32, (LANES, LANES), 0) == lax.broadcasted_iota(
-        jnp.int32, (LANES, LANES), 1
-    )
-
-    def to_lanes(column):
-        return jnp.sum(jnp.where(eye, column, 0.0), axis=0, keepdims=True)
-
-    def tile(where, count):
-        for i in range(where, where + count):
-            inner = lax.dot_general(
-                dem[...],
-                rol[pl.ds(pl.multiple_of(places[i] * blk, 16), blk), :],
-                (((1,), (1,)), ((), ())),
-                preferred_element_type=jnp.float32,
-            )
-            dist[:, i * blk : (i + 1) * blk] = (1.0 - inner) * (1.0 / EPS)
-
-    def row_stats(h, first, count, fresh):
-        def step(r, carry):
-            here = group(r)
-            values = [dist[here, lanes(c)] for c in range(first, first + count)]
-            low = tree(jnp.minimum, values)
-            if not fresh:
-                before = best[here, :]
-                low = jnp.minimum(low, before)
-            total = tree(jnp.add, [jnp.exp(low - v) for v in values])
-            if not fresh:
-                total = total + part[here, :] * jnp.exp(low - before)
-            best[here, :] = low
-            part[here, :] = total
-            return carry
-
-        over(h, step, 0, max(4, 64 // count))
-
-    def store_line(buf, index, k, line):
-        at = k * LANES
-        done = 0
-        while done < LANES:
-            i, j = (at + done) // blk, (at + done) % blk
-            n = min(LANES - done, blk - j)
-            buf[index, i : i + 1, j : j + n] = line[:, done : done + n]
-            done += n
-
-    def exchange_start(buf, index, others, ssem, rsem, h, slots):
-        here = pl.ds(h * slots, slots)
-        for i, (device, _) in enumerate(others):
-            copy = pltpu.make_async_remote_copy(
-                src_ref=buf.at[index, here],
-                dst_ref=buf.at[index, here],
-                send_sem=ssem.at[i, h],
-                recv_sem=rsem.at[index, h],
-                device_id=device,
-                device_id_type=MESH,
-            )
-            copy.start()
-            started.append(copy)
-
-    def exchange_wait(buf, others, ssem, rsem, h, slots):
-        here = pl.ds(h * slots, slots)
-        for i, (device, other) in enumerate(others):
-            pltpu.make_async_remote_copy(
-                src_ref=buf.at[other, here],
-                dst_ref=buf.at[other, here],
-                send_sem=ssem.at[i, h],
-                recv_sem=rsem.at[other, h],
-                device_id=device,
-                device_id_type=MESH,
-            ).wait_recv()
-
-    def log_total(values):
-        top = tree(jnp.maximum, values)
-        return top + jnp.log(tree(jnp.add, [jnp.exp(v - top) for v in values]))
-
-    def line_of(pieces):
-        return pieces[0] if len(pieces) == 1 else jnp.concatenate(pieces, axis=1)
-
-    def spread(h, values):
-        line = line_of([values[i : i + 1, :] for i in range(values.shape[0])])
-        for k in range(chunk // LANES):
-            column = jnp.sum(jnp.where(eye, line[:, lanes(k)], 0.0), axis=1, keepdims=True)
-            wide[lanes(h * (chunk // LANES) + k), :] = jnp.broadcast_to(column, (LANES, LANES))
-
-    per_chunk = chunk // LANES
-    slots = chunk // blk
-    log_n = math.log(plan.total)
-
-    every = [o for o in col_offsets if o[2] == 0]
-    fresh = True
-    done = 0
-    for at, (dz, dy, _) in enumerate(every):
-        if dz > 0 and dy > 0:
-            for k in range(plan.pieces):
-                index = col_peers[(dz, dy, 0)][1]
-                arrived(rol, index, k, s_rol, r_rol)
-                send_rol(index, k, partner)
-        for k in range(plan.pieces):
-            arrived(rol, col_peers[(dz, dy, 1)][1], k, s_rol, r_rol)
-        tile(2 * at, 2)
-        if (2 * (at + 1) * blk) % LANES == 0 and at + 1 < len(every):
-            upto = 2 * (at + 1) * blk // LANES
-            for h in range(chunks):
-                row_stats(h, done, upto - done, fresh)
-            fresh, done = False, upto
+                rows_in(dz, dx)
+        last_place = len(places) // 2 - 1
+        for place in range(last_place + 1):
+            cols_in(*col_offsets[2 * place][:2])
+            tile(None, place)
+            if place < last_place:
+                row_stats(0, rows, place)
+
     for h in range(chunks):
-        row_stats(h, done, n_parts - done, fresh)
+        row_stats(h * chunk, chunk, last_place)
         for k in range(h * per_chunk, (h + 1) * per_chunk):
             low = best[lanes(k), :]
             least = jnp.min(low, axis=1, keepdims=True)
@@ -318,38 +369,42 @@
             store_line(lf1, p_me, k, jnp.log(to_lanes(total)) - to_lanes(least))
         exchange_start(lf1, p_me, row_others, s_f1, r_f1, h, slots)
 
-    def col_max(r, carry):
-        here = group(r)
-        f_here = wide[here, :]
-        return tuple(
-            jnp.maximum(carry[c], f_here - dist[here, lanes(c)]) for c in range(n_parts)
-        )
-
-    tops = tuple(jnp.full((SUB, LANES), -jnp.inf, jnp.float32) for _ in range(n_parts))
+    def inside(b, g):
+        return pl.ds(pl.multiple_of(b * BLOCK + g * SUB, SUB), SUB)
+
+    def col_sum(b, carry):
+        f_here = [wide[inside(b, g), :] for g in range(GROUPS)]
+        for c in range(n_parts):
+            values = [f_here[g] - dist[inside(b, g), lanes(c)] for g in range(GROUPS)]
+            top = tree(jnp.maximum, values)
+            values = [jnp.exp(v - top) for v in values]
+            for g in range(GROUPS):
+                kern[inside(b, g), lanes(c)] = values[g]
+            tops[group(b), lanes(c)] = top
+            sums[group(b), lanes(c)] = tree(jnp.add, values)
+        return carry
+
     for h in range(chunks):
         exchange_wait(lf1, row_others, s_f1, r_f1, h, slots)
         here = pl.ds(h * slots, slots)
         f_all[here, :] = -log_n - log_total([lf1[i, here, :] for i in range(plan.gr)])
         spread(h, f_all[here, :])
-        tops = over(h, col_max, tops, 8)
-
-    def col_sum(r, carry):
-        here = group(r)
-        f_here = wide[here, :]
-        out = []
-        for c in range(n_parts):
-            value = jnp.exp((f_here - dist[here, lanes(c)]) - tops[c])
-            kern[here, lanes(c)] = value
-            out.append(carry[c] + value)
-        return tuple(out)
-
-    zeros = tuple(jnp.zeros((SUB, LANES), jnp.float32) for _ in range(n_parts))
-    sums = lax.fori_loop(0, rows // SUB, col_sum, zeros, unroll=8)
+        over(h, col_sum, 0, 1)
+
+    blocks = rows // BLOCK
     pieces = []
     for c in range(n_parts):
-        top = jnp.max(tops[c], axis=0, keepdims=True)
-        total = jnp.sum(sums[c] * jnp.exp(tops[c] - top), axis=0, keepdims=True)
-        pieces.append(top + jnp.log(total))
+        top = tree(jnp.maximum, [tops[b * SUB : (b + 1) * SUB, lanes(c)] for b in range(blocks)])
+        top = jnp.max(top, axis=0, keepdims=True)
+        total = tree(
+            jnp.add,
+            [
+                sums[b * SUB : (b + 1) * SUB, lanes(c)]
+                * jnp.exp(tops[b * SUB : (b + 1) * SUB, lanes(c)] - top)
+                for b in range(blocks)
+            ],
+        )
+        pieces.append(top + jnp.log(jnp.sum(total, axis=0, keepdims=True)))
     line = line_of(pieces)
     for i, place in enumerate(places):
         lg[q_me, pl.ds(place, 1), :] = line[:, i * blk : (i + 1) * blk]
@@ -358,51 +413,53 @@
     g_all[...] = -log_n - log_total([lg[i] for i in range(plan.gc)])
     g_line = line_of([g_all[pl.ds(place, 1), :] for place in places])
     for c in range(n_parts):
-        scale[:, lanes(c)] = jnp.exp(tops[c] + g_line[:, lanes(c)])
-
-    def second_rows(r, carry):
-        here = group(r)
-        part[here, :] = tree(
-            jnp.add, [kern[here, lanes(c)] * scale[:, lanes(c)] for c in range(n_parts)]
-        )
+        tops[:, lanes(c)] = jnp.exp(tops[:, lanes(c)] + g_line[:, lanes(c)])
+
+    def second_rows(b, carry):
+        totals = [None] * GROUPS
+        for c in range(n_parts):
+            scale = tops[group(b), lanes(c)]
+            for g in range(GROUPS):
+                value = kern[inside(b, g), lanes(c)] * scale
+                totals[g] = value if c == 0 else totals[g] + value
+        for g in range(GROUPS):
+            part[inside(b, g), :] = totals[g]
         return carry
 
     for h in range(chunks):
-        over(h, second_rows, 0, 8)
+        over(h, second_rows, 0, 1)
         for k in range(h * per_chunk, (h + 1) * per_chunk):
             total = jnp.sum(part[lanes(k), :], axis=1, keepdims=True)
             store_line(lf2, p_me, k, to_lanes(total))
         exchange_start(lf2, p_me, row_others, s_f2, r_f2, h, slots)
 
-    def last(r, carry):
-        here = group(r)
-        u_here = wide[here, :]
-        mass_c, cost_c = carry
-        new_mass, new_cost = [], []
+    def last(b, carry):
+        u_here = [wide[inside(b, g), :] for g in range(GROUPS)]
         for c in range(n_parts):
-            value = u_here * kern[here, lanes(c)]
-            new_mass.append(mass_c[c] + value)
-            new_cost.append(cost_c[c] + value * dist[here, lanes(c)])
-        return tuple(new_mass), tuple(new_cost)
-
-    both = (zeros, zeros)
+            scale = tops[group(b), lanes(c)]
+            values = [u_here[g] * kern[inside(b, g), lanes(c)] for g in range(GROUPS)]
+            mass_c[:, lanes(c)] += tree(jnp.add, values) * scale
+            values = [values[g] * dist[inside(b, g), lanes(c)] for g in range(GROUPS)]
+            cost_c[:, lanes(c)] += tree(jnp.add, values) * scale
+        return carry
+
+    mass_c[...] = jnp.zeros_like(mass_c)
+    cost_c[...] = jnp.zeros_like(cost_c)
     for h in range(chunks):
         exchange_wait(lf2, row_others, s_f2, r_f2, h, slots)
         here = pl.ds(h * slots, slots)
         mass = tree(jnp.add, [lf2[i, here, :] for i in range(plan.gr)]) * float(plan.total)
         spread(h, 1.0 / mass)
         f_all[here, :] = f_all[here, :] - jnp.log(mass)
-        both = over(h, last, both, 4)
-
-    def finish(values):
-        return line_of(
-            [
-                jnp.sum(values[c] * scale[:, lanes(c)], axis=0, keepdims=True)
-                for c in range(n_parts)
-            ]
-        )
-
-    both = jnp.concatenate([finish(both[0]), finish(both[1])], axis=0)
+        over(h, last, 0, 1)
+
+    both = jnp.concatenate(
+        [
+            jnp.sum(mass_c[...], axis=0, keepdims=True),
+            jnp.sum(cost_c[...], axis=0, keepdims=True),
+        ],
+        axis=0,
+    )
     for i, place in enumerate(places):
         cw_out[place] = both[:, i * blk : (i + 1) * blk]
     for i, (device, other) in enumerate(col_others):
@@ -457,6 +514,9 @@
             pltpu.VMEM((rows, LANES), f32),
             pltpu.VMEM((rows, LANES), f32),
             pltpu.VMEM((rows, LANES), f32),
+            pltpu.VMEM((rows // GROUPS, cols), f32),
+            pltpu.VMEM((rows // GROUPS, cols), f32),
+            pltpu.VMEM((SUB, cols), f32),
             pltpu.VMEM((SUB, cols), f32),
             pltpu.VMEM((plan.gr, plan.gr, blk), f32),
             pltpu.VMEM((plan.gr, plan.gr, blk), f32),

time: 43.6 us -> 42.9 us (0.984)
  Pallas kernels: 41.5 us -> 40.7 us
    pallas_call x1, Pallas kernels: 41.5 us -> 40.7 us  [body(): pl.pallas_call(functools.partial(kernel, plan), out_shape=jax.ShapeDtypeS...]
where the time goes in v4:
time: 42.9 us; the launch traced here: 42.7 us
  Pallas kernels  40.7 us (95%)
  local copies, waits for them, and re-layouts  1.36 us (3%)
  between operations  0.64 us (1%)
    pallas_call x1, Pallas kernels, body(): pl.pallas_call(functools.partial(kernel, plan), out_shape=jax.ShapeDtypeS...  40.7 us
    slice x1, local copies, waits for them, and re-layouts, body(): return (out[0], out[1], out[2])  1.36 us

profile of v4, /device:TPU:0, one launch (start us, length us, event | category | flops | bytes accessed | tf_op | source)
XLA Modules:
  0.0 42.7 jit_solution(10636754806484207652)
XLA Ops:
  0.6 40.7 %shard_map.49 = f32[3,256]{1,0:T(4,128)} custom-call(bf16[256,256]{1,0:T(8,128)(2,1)} %demo_hbm.1, bf16[256,256]{1,0:T(8,128)(2,1)} %roll_hbm.1), custom_call_target="tpu_custom_call" | custom-call | tf_op jit(solution)/shard_map/pallas_call | solution.py:502
  41.4 1.4 %fusion = (f32[1,256]{1,0:T(1,128)}, f32[1,256]{1,0:T(1,128)}, f32[1,256]{1,0:T(1,128)}) fusion(f32[3,256]{1,0:T(4,128)} %shard_map.49), kind=kLoop, calls=%fused_computation | loop fusion | bytes 6144 | tf_op jit(solution)/shard_map/slice | solution.py:546

commit v5 on v4

v5 whole, which is shorter than its diff:
```python
import functools
import math

import jax
import jax.numpy as jnp
from jax import lax
from jax.experimental import pallas as pl
from jax.experimental.pallas import tpu as pltpu
from jax.sharding import PartitionSpec as P

EPS = 0.005
MESH = pl.DeviceIdType.MESH
LANES = 128
SUB = 8
GROUPS = 8
BLOCK = SUB * GROUPS


class Plan:
    def __init__(self, rows_axis, cols_axis, blk, width):
        self.core = 2
        depth = rows_axis // 2
        self.x = 1 << ((cols_axis.bit_length() - 1) // 2)
        self.y = cols_axis // self.x
        self.zl = min(depth, max(1, cols_axis // self.x))
        self.zh = depth // self.zl
        self.blk = blk
        self.width = width
        self.gr = self.zl * self.x
        self.gc = self.zh * self.y * self.core
        self.rows = self.gr * blk
        self.cols = self.gc * blk
        self.total = rows_axis * cols_axis * blk
        self.pieces = max(1, min(4, blk // 16))
        self.piece = blk // self.pieces
        self.chunks = 2 if blk % LANES == 0 and self.gr % 2 == 0 else 1


def normalize(embed):
    values = embed.astype(jnp.float32)
    inverse = lax.rsqrt(jnp.sum(values * values, axis=-1, keepdims=True) + 1e-06)
    return (values * inverse).astype(jnp.bfloat16)


def tree(op, items):
    items = list(items)
    while len(items) > 1:
        items = [
            op(items[i], items[i + 1]) if i + 1 < len(items) else items[i]
            for i in range(0, len(items), 2)
        ]
    return items[0]


def kernel(
    plan,
    demo_hbm,
    roll_hbm,
    out_ref,
    demo_ref,
    roll_ref,
    dem,
    rol,
    dist,
    kern,
    best,
    part,
    wide,
    tops,
    sums,
    mass_c,
    cost_c,
    lf1,
    lf2,
    lg,
    f_all,
    g_all,
    cw_out,
    cw_in,
    s_in,
    s_dem,
    r_dem,
    s_rol,
    r_rol,
    s_f1,
    r_f1,
    s_f2,
    r_f2,
    s_g,
    r_g,
    s_c,
    r_c,
):
    blk, rows, cols = plan.blk, plan.rows, plan.cols
    n_parts = cols // LANES
    chunks, chunk = plan.chunks, rows // plan.chunks
    row = lax.axis_index("row")
    col = lax.axis_index("col")
    core, z = lax.rem(row, 2), row // 2
    zlo, zhi = lax.rem(z, plan.zl), z // plan.zl
    x, y = lax.rem(col, plan.x), col // plan.x

    load_demo = pltpu.make_async_copy(demo_hbm, demo_ref, s_in.at[0])
    load_roll = pltpu.make_async_copy(roll_hbm, roll_ref, s_in.at[1])
    load_demo.start()
    load_roll.start()

    def row_peer(dz, dx):
        zz, xx = lax.rem(zlo + dz, plan.zl), lax.rem(x + dx, plan.x)
        device = ((zhi * plan.zl + zz) * 2 + core, y * plan.x + xx)
        return device, zz * plan.x + xx

    def col_peer(dz, dy, dc):
        zz, yy, cc = lax.rem(zhi + dz, plan.zh), lax.rem(y + dy, plan.y), lax.rem(core + dc, 2)
        device = ((zz * plan.zl + zlo) * 2 + cc, yy * plan.x + x)
        return device, (zz * plan.y + yy) * 2 + cc

    row_offsets = [(a, b) for a in range(plan.zl) for b in range(plan.x)]
    col_offsets = [(a, b, c) for a in range(plan.zh) for b in range(plan.y) for c in range(2)]
    row_peers = {o: row_peer(*o) for o in row_offsets}
    col_peers = {o: col_peer(*o) for o in col_offsets}
    p_me = row_peers[(0, 0)][1]
    q_me = col_peers[(0, 0, 0)][1]
    row_others = [row_peers[o] for o in row_offsets[1:]]
    col_others = [col_peers[o] for o in col_offsets[1:]]
    places = [col_peers[o][1] for o in col_offsets]

    barrier = pltpu.get_barrier_semaphore()
    for device, _ in row_others + col_others:
        pl.semaphore_signal(barrier, inc=1, device_id=device, device_id_type=MESH)

    def slot(buf, index, piece):
        start = pl.multiple_of(index * blk + piece * plan.piece, 16)
        return buf.at[pl.ds(start, plan.piece), :]

    load_demo.wait()
    dem[pl.ds(pl.multiple_of(p_me * blk, 16), blk), :] = normalize(demo_ref[...])
    load_roll.wait()
    rol[pl.ds(pl.multiple_of(q_me * blk, 16), blk), :] = normalize(roll_ref[...])
    pl.semaphore_wait(barrier, len(row_others) + len(col_others))

    partner = col_peers[(0, 0, 1)][0]
    started = []
    per_dem = (plan.zl - 1) + (plan.x - 1) * plan.zl
    per_rol = (plan.zh - 1) + (plan.y - 1) * plan.zh + plan.zh * plan.y

    def send(buf, index, piece, device, ssem, rsem, number):
        ref = slot(buf, index, piece)
        pltpu.make_async_remote_copy(
            src_ref=ref,
            dst_ref=ref,
            send_sem=ssem.at[number],
            recv_sem=rsem.at[index, piece],
            device_id=device,
            device_id_type=MESH,
        ).start()

    def arrived(buf, index, piece, ssem, rsem):
        ref = slot(buf, index, piece)
        pltpu.make_async_remote_copy(
            src_ref=ref,
            dst_ref=ref,
            send_sem=ssem.at[0],
            recv_sem=rsem.at[index, piece],
            device_id=partner,
            device_id_type=MESH,
        ).wait_recv()

    def each_piece(run):
        def step(k, carry):
            counts = [k * per_dem, k * per_rol]

            def dem_on(index, device):
                send(dem, index, k, device, s_dem, r_dem, counts[0])
                counts[0] += 1

            def rol_on(index, device):
                send(rol, index, k, device, s_rol, r_rol, counts[1])
                counts[1] += 1

            run(k, counts, dem_on, rol_on)
            return carry

        lax.fori_loop(0, plan.pieces, step, 0)

    def first_hop(k, counts, dem_on, rol_on):
        for dz in range(1, plan.zl):
            dem_on(p_me, row_peers[(dz, 0)][0])
        for dz in range(1, plan.zh):
            rol_on(q_me, col_peers[(dz, 0, 0)][0])
        for dx in range(1, plan.x):
            dem_on(p_me, row_peers[(0, dx)][0])
        for dy in range(1, plan.y):
            rol_on(q_me, col_peers[(0, dy, 0)][0])
        rol_on(q_me, partner)

    first_dem = (plan.zl - 1) + (plan.x - 1)
    first_rol = (plan.zh - 1) + (plan.y - 1) + 1

    def second_hop(k, counts, dem_on, rol_on):
        counts[0] += first_dem
        counts[1] += first_rol
        for dz in range(1, plan.zl):
            index = row_peers[(dz, 0)][1]
            arrived(dem, index, k, s_dem, r_dem)
            for dx in range(1, plan.x):
                dem_on(index, row_peers[(0, dx)][0])
        for dz in range(1, plan.zh):
            index = col_peers[(dz, 0, 0)][1]
            arrived(rol, index, k, s_rol, r_rol)
            for dy in range(1, plan.y):
                rol_on(index, col_peers[(0, dy, 0)][0])
            rol_on(index, partner)
        for dy in range(1, plan.y):
            index = col_peers[(0, dy, 0)][1]
            arrived(rol, index, k, s_rol, r_rol)
            rol_on(index, partner)

    second_rol = (plan.zh - 1) * plan.y + (plan.y - 1)

    def relay(k, counts, dem_on, rol_on):
        counts[1] += first_rol + second_rol
        for dz in range(1, plan.zh):
            for dy in range(1, plan.y):
                index = col_peers[(dz, dy, 0)][1]
                arrived(rol, index, k, s_rol, r_rol)
                rol_on(index, partner)
        for dz in range(plan.zl):
            for dx in range(1, plan.x):
                arrived(dem, row_peers[(dz, dx)][1], k, s_dem, r_dem)

    each_piece(first_hop)
    each_piece(second_hop)
    each_piece(relay)

    def lanes(c):
        return slice(c * LANES, (c + 1) * LANES)

    def group(r):
        return pl.ds(pl.multiple_of(r * SUB, SUB), SUB)

    def over(h, body, init, unroll):
        first = h * (chunk // BLOCK)
        return lax.fori_loop(first, first + chunk // BLOCK, body, init, unroll=unroll)

    eye = lax.broadcasted_iota(jnp.int32, (LANES, LANES), 0) == lax.broadcasted_iota(
        jnp.int32, (LANES, LANES), 1
    )

    def to_lanes(column):
        return jnp.sum(jnp.where(eye, column, 0.0), axis=0, keepdims=True)

    pair = 2 * blk // LANES

    def at(here, c):
        return dist[c // pair, here, lanes(c % pair)]

    def columns(place, carry):
        zz, yy = lax.rem(zhi + place // plan.y, plan.zh), lax.rem(y + place % plan.y, plan.y)
        index = (zz * plan.y + yy) * 2

        def piece_in(k, c):
            arrived(rol, index + (1 - core), k, s_rol, r_rol)
            return c

        lax.fori_loop(0, plan.pieces, piece_in, 0)

        def unit(where, carry):
            first = pl.multiple_of(where * blk, 16)
            for c in range(2):
                other = index + (core if c == 0 else 1 - core)
                inner = lax.dot_general(
                    dem[pl.ds(first, blk), :],
                    rol[pl.ds(pl.multiple_of(other * blk, 16), blk), :],
                    (((1,), (1,)), ((), ())),
                    preferred_element_type=jnp.float32,
                )
                dist[place, pl.ds(first, blk), c * blk : (c + 1) * blk] = (1.0 - inner) * (
                    1.0 / EPS
                )

            def step(r, carry):
                here = pl.ds(pl.multiple_of(first + r * SUB, SUB), SUB)
                values = [dist[place, here, lanes(c)] for c in range(pair)]
                before = best[here, :]
                low = jnp.minimum(before, tree(jnp.minimum, values))
                total = tree(jnp.add, [jnp.exp(low - v) for v in values])
                part[here, :] = total + part[here, :] * jnp.exp(low - before)
                best[here, :] = low
                return carry

            return lax.fori_loop(0, blk // SUB, step, carry, unroll=min(16, blk // SUB))

        return lax.fori_loop(0, plan.gr, unit, carry)

    def store_line(buf, index, first, k, line):
        at = k * LANES
        done = 0
        while done < LANES:
            i, j = (at + done) // blk, (at + done) % blk
            n = min(LANES - done, blk - j)
            buf[index, first, i : i + 1, j : j + n] = line[:, done : done + n]
            done += n

    def shared(buf, index, device, ssem, rsem, i, h):
        ref = buf.at[index, h]
        return pltpu.make_async_remote_copy(
            src_ref=ref,
            dst_ref=ref,
            send_sem=ssem.at[i, h],
            recv_sem=rsem.at[index, h],
            device_id=device,
            device_id_type=MESH,
        )

    def exchange_start(buf, index, others, ssem, rsem, h):
        for i, (device, _) in enumerate(others):
            shared(buf, index, device, ssem, rsem, i, h).start()

    def exchange_wait(buf, others, ssem, rsem, h):
        for i, (device, other) in enumerate(others):
            shared(buf, other, device, ssem, rsem, i, h).wait_recv()

    def exchange_sent(buf, index, others, ssem, rsem, h):
        for i, (device, _) in enumerate(others):
            shared(buf, index, device, ssem, rsem, i, h).wait_send()

    def log_total(values):
        top = tree(jnp.maximum, values)
        return top + jnp.log(tree(jnp.add, [jnp.exp(v - top) for v in values]))

    def line_of(pieces):
        return pieces[0] if len(pieces) == 1 else jnp.concatenate(pieces, axis=1)

    def spread(h, values):
        line = line_of([values[i : i + 1, :] for i in range(values.shape[0])])
        for k in range(chunk // LANES):
            column = jnp.sum(jnp.where(eye, line[:, lanes(k)], 0.0), axis=1, keepdims=True)
            start = pl.multiple_of(h * chunk + k * LANES, LANES)
            wide[pl.ds(start, LANES), :] = jnp.broadcast_to(column, (LANES, LANES))

    per_chunk = chunk // LANES
    slots = chunk // blk
    log_n = math.log(plan.total)

    def each_chunk(run):
        def step(h, carry):
            run(h)
            return carry

        lax.fori_loop(0, chunks, step, 0)

    best[...] = jnp.full_like(best, 1e30)
    part[...] = jnp.zeros_like(part)
    lax.fori_loop(0, plan.zh * plan.y, columns, 0)

    def first_f(h):
        for k in range(per_chunk):
            here = pl.ds(pl.multiple_of(h * chunk + k * LANES, LANES), LANES)
            low = best[here, :]
            least = jnp.min(low, axis=1, keepdims=True)
            total = jnp.sum(part[here, :] * jnp.exp(least - low), axis=1, keepdims=True)
            store_line(lf1, p_me, h, k, jnp.log(to_lanes(total)) - to_lanes(least))
        exchange_start(lf1, p_me, row_others, s_f1, r_f1, h)

    each_chunk(first_f)

    def inside(b, g):
        return pl.ds(pl.multiple_of(b * BLOCK + g * SUB, SUB), SUB)

    def col_sum(b, carry):
        f_here = [wide[inside(b, g), :] for g in range(GROUPS)]
        for c in range(n_parts):
            values = [f_here[g] - at(inside(b, g), c) for g in range(GROUPS)]
            top = tree(jnp.maximum, values)
            values = [jnp.exp(v - top) for v in values]
            for g in range(GROUPS):
                kern[inside(b, g), lanes(c)] = values[g]
            tops[group(b), lanes(c)] = top
            sums[group(b), lanes(c)] = tree(jnp.add, values)
        return carry

    def first_g(h):
        exchange_wait(lf1, row_others, s_f1, r_f1, h)
        f_all[h] = -log_n - log_total([lf1[i, h] for i in range(plan.gr)])
        spread(h, f_all[h])
        over(h, col_sum, 0, 1)

    each_chunk(first_g)
    blocks = rows // BLOCK
    low_all = tuple(jnp.full((SUB, LANES), -1e30, jnp.float32) for _ in range(n_parts))
    top_all = lax.fori_loop(
        0,
        blocks,
        lambda b, m: tuple(jnp.maximum(m[c], tops[group(b), lanes(c)]) for c in range(n_parts)),
        low_all,
        unroll=4,
    )
    sum_all = lax.fori_loop(
        0,
        blocks,
        lambda b, t: tuple(
            t[c] + sums[group(b), lanes(c)] * jnp.exp(tops[group(b), lanes(c)] - top_all[c])
            for c in range(n_parts)
        ),
        tuple(jnp.zeros((SUB, LANES), jnp.float32) for _ in range(n_parts)),
        unroll=4,
    )
    pieces = []
    for c in range(n_parts):
        top = jnp.max(top_all[c], axis=0, keepdims=True)
        total = jnp.sum(sum_all[c] * jnp.exp(top_all[c] - top), axis=0, keepdims=True)
        pieces.append(top + jnp.log(total))
    line = line_of(pieces)
    for i, place in enumerate(places):
        lg[q_me, 0, pl.ds(place, 1), :] = line[:, i * blk : (i + 1) * blk]
    exchange_start(lg, q_me, col_others, s_g, r_g, 0)
    exchange_wait(lg, col_others, s_g, r_g, 0)
    g_all[...] = -log_n - log_total([lg[i, 0] for i in range(plan.gc)])
    g_line = line_of([g_all[pl.ds(place, 1), :] for place in places])

    def rescale(b, carry):
        tops[group(b), :] = jnp.exp(tops[group(b), :] + g_line)
        return carry

    lax.fori_loop(0, blocks, rescale, 0, unroll=4)

    def second_rows(b, carry):
        totals = [None] * GROUPS
        for c in range(n_parts):
            scale = tops[group(b), lanes(c)]
            for g in range(GROUPS):
                value = kern[inside(b, g), lanes(c)] * scale
                totals[g] = value if c == 0 else totals[g] + value
        for g in range(GROUPS):
            part[inside(b, g), :] = totals[g]
        return carry

    def second_f(h):
        over(h, second_rows, 0, 1)
        for k in range(per_chunk):
            here = pl.ds(pl.multiple_of(h * chunk + k * LANES, LANES), LANES)
            total = jnp.sum(part[here, :], axis=1, keepdims=True)
            store_line(lf2, p_me, h, k, to_lanes(total))
        exchange_start(lf2, p_me, row_others, s_f2, r_f2, h)

    each_chunk(second_f)

    def last(b, carry):
        u_here = [wide[inside(b, g), :] for g in range(GROUPS)]
        for c in range(n_parts):
            scale = tops[group(b), lanes(c)]
            values = [u_here[g] * kern[inside(b, g), lanes(c)] for g in range(GROUPS)]
            mass_c[:, lanes(c)] += tree(jnp.add, values) * scale
            values = [values[g] * at(inside(b, g), c) for g in range(GROUPS)]
            cost_c[:, lanes(c)] += tree(jnp.add, values) * scale
        return carry

    mass_c[...] = jnp.zeros_like(mass_c)
    cost_c[...] = jnp.zeros_like(cost_c)

    def second_g(h):
        exchange_wait(lf2, row_others, s_f2, r_f2, h)
        mass = tree(jnp.add, [lf2[i, h] for i in range(plan.gr)]) * float(plan.total)
        spread(h, 1.0 / mass)
        f_all[h] = f_all[h] - jnp.log(mass)
        over(h, last, 0, 1)

    each_chunk(second_g)
    both = jnp.concatenate(
        [
            jnp.sum(mass_c[...], axis=0, keepdims=True),
            jnp.sum(cost_c[...], axis=0, keepdims=True),
        ],
        axis=0,
    )
    for i, place in enumerate(places):
        cw_out[place] = both[:, i * blk : (i + 1) * blk]
    for i, (device, other) in enumerate(col_others):
        copy = pltpu.make_async_remote_copy(
            src_ref=cw_out.at[other],
            dst_ref=cw_in.at[q_me],
            send_sem=s_c.at[i],
            recv_sem=r_c.at[q_me],
            device_id=device,
            device_id_type=MESH,
        )
        copy.start()
        started.append(copy)
    cw_in[q_me] = cw_out[q_me]
    for i, (device, other) in enumerate(col_others):
        pltpu.make_async_remote_copy(
            src_ref=cw_out.at[other],
            dst_ref=cw_in.at[other],
            send_sem=s_c.at[i],
            recv_sem=r_c.at[other],
            device_id=device,
            device_id_type=MESH,
        ).wait_recv()
    total = tree(jnp.add, [cw_in[i] for i in range(plan.gc)])
    out_ref[0:1, :] = f_all[p_me // slots, pl.ds(lax.rem(p_me, slots), 1), :]
    out_ref[1:2, :] = g_all[pl.ds(q_me, 1), :] - jnp.log(total[0:1] * float(plan.total))
    out_ref[2:3, :] = total[1:2] / total[0:1] * -EPS
    for copy in started:
        copy.wait_send()
    for h in range(chunks):
        exchange_sent(lf1, p_me, row_others, s_f1, r_f1, h)
        exchange_sent(lf2, p_me, row_others, s_f2, r_f2, h)
    exchange_sent(lg, q_me, col_others, s_g, r_g, 0)

    def sent(buf, index, ssem, rsem, count):
        ref = slot(buf, index, 0)

        def step(i, carry):
            pltpu.make_async_remote_copy(
                src_ref=ref,
                dst_ref=ref,
                send_sem=ssem.at[i],
                recv_sem=rsem.at[index, 0],
                device_id=partner,
                device_id_type=MESH,
            ).wait_send()
            return carry

        lax.fori_loop(0, count, step, 0)

    sent(dem, p_me, s_dem, r_dem, plan.pieces * per_dem)
    sent(rol, q_me, s_rol, r_rol, plan.pieces * per_rol)


def body(plan, demo, rollout):
    blk, width, rows, cols = plan.blk, plan.width, plan.rows, plan.cols
    n_dem = plan.pieces * ((plan.zl - 1) + (plan.x - 1) * plan.zl)
    n_rol = plan.pieces * (
        (plan.zh - 1) + (plan.y - 1) * plan.zh + plan.zh * plan.y
    )
    dma = pltpu.SemaphoreType.DMA
    f32 = jnp.float32
    out = pl.pallas_call(
        functools.partial(kernel, plan),
        out_shape=jax.ShapeDtypeStruct((3, blk), f32),
        in_specs=[pl.BlockSpec(memory_space=pltpu.HBM)] * 2,
        out_specs=pl.BlockSpec(memory_space=pltpu.VMEM),
        scratch_shapes=[
            pltpu.VMEM((blk, width), jnp.bfloat16),
            pltpu.VMEM((blk, width), jnp.bfloat16),
            pltpu.VMEM((rows, width), jnp.bfloat16),
            pltpu.VMEM((cols, width), jnp.bfloat16),
            pltpu.VMEM((plan.zh * plan.y, rows, 2 * blk), f32),
            pltpu.VMEM((rows, cols), f32),
            pltpu.VMEM((rows, LANES), f32),
            pltpu.VMEM((rows, LANES), f32),
            pltpu.VMEM((rows, LANES), f32),
            pltpu.VMEM((rows // GROUPS, cols), f32),
            pltpu.VMEM((rows // GROUPS, cols), f32),
            pltpu.VMEM((SUB, cols), f32),
            pltpu.VMEM((SUB, cols), f32),
            pltpu.VMEM((plan.gr, plan.chunks, plan.gr // plan.chunks, blk), f32),
            pltpu.VMEM((plan.gr, plan.chunks, plan.gr // plan.chunks, blk), f32),
            pltpu.VMEM((plan.gc, 1, plan.gc, blk), f32),
            pltpu.VMEM((plan.chunks, plan.gr // plan.chunks, blk), f32),
            pltpu.VMEM((plan.gc, blk), f32),
            pltpu.VMEM((plan.gc, 2, blk), f32),
            pltpu.VMEM((plan.gc, 2, blk), f32),
            dma((2,)),
            dma((n_dem,)),
            dma((plan.gr, plan.pieces)),
            dma((n_rol,)),
            dma((plan.gc, plan.pieces)),
            dma((plan.gr, plan.chunks)),
            dma((plan.gr, plan.chunks)),
            dma((plan.gr, plan.chunks)),
            dma((plan.gr, plan.chunks)),
            dma((plan.gc, 1)),
            dma((plan.gc, 1)),
            dma((plan.gc,)),
            dma((plan.gc,)),
        ],
        compiler_params=pltpu.CompilerParams(
            collective_id=0, has_side_effects=True, vmem_limit_bytes=64 * 1024 * 1024 - 128 * 1024
        ),
    )(demo, rollout)
    return out[0], out[1], out[2]


def solution(mesh):
    rows_axis, cols_axis = mesh.shape["row"], mesh.shape["col"]

    def run(demo, rollout):
        blk = demo.shape[0] // (rows_axis * cols_axis)
        plan = Plan(rows_axis, cols_axis, blk, demo.shape[1])
        return jax.shard_map(
            functools.partial(body, plan),
            mesh=mesh,
            in_specs=(P(("row", "col"), None), P(("row", "col"), None)),
            out_specs=(P(("row", "col")), P(("row", "col")), P(("row", "col"))),
            check_vma=False,
        )(demo, rollout)

    return run
```

time: 42.9 us -> 45.8 us (1.068)
  Pallas kernels: 40.7 us -> 43.7 us
    pallas_call x1, Pallas kernels: 40.7 us -> 43.7 us  [body(): pl.pallas_call(functools.partial(kernel, plan), out_shape=jax.ShapeDtypeS...]
where the time goes in v5:
time: 45.8 us; the launch traced here: 45.7 us
  Pallas kernels  43.7 us (95%)
  local copies, waits for them, and re-layouts  1.36 us (3%)
  between operations  0.64 us (1%)
    pallas_call x1, Pallas kernels, body(): pl.pallas_call(functools.partial(kernel, plan), out_shape=jax.ShapeDtypeS...  43.7 us
    slice x1, local copies, waits for them, and re-layouts, body(): return (out[0], out[1], out[2])  1.36 us

profile of v5, /device:TPU:0, one launch (start us, length us, event | category | flops | bytes accessed | tf_op | source)
XLA Modules:
  0.0 45.7 jit_solution(16872962016674076775)
XLA Ops:
  0.6 43.7 %shard_map.49 = f32[3,256]{1,0:T(4,128)} custom-call(bf16[256,256]{1,0:T(8,128)(2,1)} %demo_hbm.1, bf16[256,256]{1,0:T(8,128)(2,1)} %roll_hbm.1), custom_call_target="tpu_custom_call" | custom-call | tf_op jit(solution)/shard_map/pallas_call | solution.py:539
  44.3 1.4 %fusion = (f32[1,256]{1,0:T(1,128)}, f32[1,256]{1,0:T(1,128)}, f32[1,256]{1,0:T(1,128)}) fusion(f32[3,256]{1,0:T(4,128)} %shard_map.49), kind=kLoop, calls=%fused_computation | loop fusion | bytes 6144 | tf_op jit(solution)/shard_map/slice | solution.py:583

commit v6 on v4

--- a/solution.py
+++ b/solution.py
@@ -191,12 +191,14 @@
         first = h * chunk // BLOCK
         return lax.fori_loop(first, first + chunk // BLOCK, body, init, unroll=unroll)
 
-    eye = lax.broadcasted_iota(jnp.int32, (LANES, LANES), 0) == lax.broadcasted_iota(
-        jnp.int32, (LANES, LANES), 1
-    )
-
-    def to_lanes(column):
-        return jnp.sum(jnp.where(eye, column, 0.0), axis=0, keepdims=True)
+    def total_line(k, size):
+        return lax.dot_general(
+            jnp.ones((SUB, LANES), jnp.float32),
+            part[k * LANES : k * LANES + size, :],
+            (((1,), (1,)), ((), ())),
+            precision=lax.Precision.HIGHEST,
+            preferred_element_type=jnp.float32,
+        )[0:1, :]
 
     def tile(where, place):
         first = 0 if where is None else pl.multiple_of(where * blk, 16)
@@ -277,9 +279,14 @@
 
     def spread(h, values):
         line = line_of([values[i : i + 1, :] for i in range(values.shape[0])])
-        for k in range(chunk // LANES):
-            column = jnp.sum(jnp.where(eye, line[:, lanes(k)], 0.0), axis=1, keepdims=True)
-            wide[lanes(h * (chunk // LANES) + k), :] = jnp.broadcast_to(column, (LANES, LANES))
+        first = lax.broadcasted_iota(jnp.int32, (SUB, chunk), 0) == 0
+        wide[h * chunk : (h + 1) * chunk, :] = lax.dot_general(
+            jnp.where(first, line, 0.0),
+            jnp.ones((SUB, LANES), jnp.float32),
+            (((0,), (0,)), ((), ())),
+            precision=lax.Precision.HIGHEST,
+            preferred_element_type=jnp.float32,
+        )
 
     per_chunk = chunk // LANES
     slots = chunk // blk
@@ -363,10 +370,10 @@
     for h in range(chunks):
         row_stats(h * chunk, chunk, last_place)
         for k in range(h * per_chunk, (h + 1) * per_chunk):
-            low = best[lanes(k), :]
-            least = jnp.min(low, axis=1, keepdims=True)
-            total = jnp.sum(part[lanes(k), :] * jnp.exp(least - low), axis=1, keepdims=True)
-            store_line(lf1, p_me, k, jnp.log(to_lanes(total)) - to_lanes(least))
+            low = best[lanes(k), :].T
+            least = jnp.min(low, axis=0, keepdims=True)
+            total = jnp.sum(part[lanes(k), :].T * jnp.exp(least - low), axis=0, keepdims=True)
+            store_line(lf1, p_me, k, jnp.log(total) - least)
         exchange_start(lf1, p_me, row_others, s_f1, r_f1, h, slots)
 
     def inside(b, g):
@@ -428,9 +435,9 @@
 
     for h in range(chunks):
         over(h, second_rows, 0, 1)
-        for k in range(h * per_chunk, (h + 1) * per_chunk):
-            total = jnp.sum(part[lanes(k), :], axis=1, keepdims=True)
-            store_line(lf2, p_me, k, to_lanes(total))
+        line = total_line(h * per_chunk, chunk)
+        for k in range(per_chunk):
+            store_line(lf2, p_me, h * per_chunk + k, line[:, lanes(k)])
         exchange_start(lf2, p_me, row_others, s_f2, r_f2, h, slots)
 
     def last(b, carry):
@@ -540,9 +547,12 @@
             dma((plan.gc,)),
         ],
         compiler_params=pltpu.CompilerParams(
-            collective_id=0, has_side_effects=True, vmem_limit_bytes=64 * 1024 * 1024 - 128 * 1024
+            collective_id=0, has_side_effects=True, vmem_limit_bytes=48 * 1024 * 1024
         ),
-    )(demo, rollout)
+    )(
+        pltpu.with_memory_space_constraint(demo, pltpu.HBM),
+        pltpu.with_memory_space_constraint(rollout, pltpu.HBM),
+    )
     return out[0], out[1], out[2]
 
 

time: 42.9 us -> 43.6 us (1.016)
  Pallas kernels: 40.7 us -> 42.2 us
  local copies, waits for them, and re-layouts: 1.36 us -> 0.57 us
    pallas_call x1, Pallas kernels: 40.7 us -> 42.2 us  [body(): pl.pallas_call(functools.partial(kernel, plan), out_shape=jax.ShapeDtypeS...]
    slice x1, local copies, waits for them, and re-layouts: 1.36 us -> 0.57 us  [body(): return (out[0], out[1], out[2])]
where the time goes in v6:
time: 43.6 us; the launch traced here: 43.4 us
  Pallas kernels  42.2 us (97%)
  between operations  0.64 us (1%)
  local copies, waits for them, and re-layouts  0.57 us (1%)
    pallas_call x1, Pallas kernels, body(): pl.pallas_call(functools.partial(kernel, plan), out_shape=jax.ShapeDtypeS...  42.2 us

profile of v6, /device:TPU:0, one launch (start us, length us, event | category | flops | bytes accessed | tf_op | source)
XLA Modules:
  0.0 43.4 jit_solution(11944026783080070982)
XLA Ops:
  0.6 42.2 %shard_map.49 = f32[3,256]{1,0:T(4,128)S(1)} custom-call(bf16[256,256]{1,0:T(8,128)(2,1)} %demo_hbm.1, bf16[256,256]{1,0:T(8,128)(2,1)} %roll_hbm.1), custom_call_target="tpu_custom_call" | custom-call | tf_op jit(solution)/shard_map/pallas_call | solution.py:509
  42.8 0.6 %fusion = (f32[1,256]{1,0:T(1,128)}, f32[1,256]{1,0:T(1,128)}, f32[1,256]{1,0:T(1,128)}) fusion(f32[3,256]{1,0:T(4,128)S(1)} %shard_map.49), kind=kLoop, calls=%fused_computation | loop fusion | bytes 6144 | tf_op jit(solution)/shard_map/slice | solution.py:556
